TPU v7x, 512 devices: a whole 4x4x16 slice. The times are simulated.
512 devices in a mesh: traj: 128 (over y, z, core), var: 4 (over x).
Axes of the slice: x: 4, y: 4, z: 16, core: 2. Of those that a mesh axis runs over, the one named last changes fastest.
Arguments:
- series: bfloat16 [393216, 1024], P('traj', 'var'), may hold values from -6 to 6
- lengths: int32 [512], P('traj'), may hold values from 64 to 2048, as said below
- tile_owner: int32 [3072], P('traj'), may hold values from 0 to 4, as said below
- factor_h: float32 [64, 64], replicated, as said below
- factor_v: float32 [64, 1024], P(None, 'var'), may hold values from -6 to 6
- weights_s: float32 [64, 512], P(None, 'traj'), may hold values from 0.5 to 2
Outputs:
- new_h: float32 [64, 64], replicated
- new_v: float32 [64, 1024], P(None, 'var')
- new_s: float32 [64, 512], P(None, 'traj')
Inputs may be any that keep to these rules, and one draw needn't show every extreme that they name: `lengths`: each length is a multiple of 64 and needs at most 1 + (length - 1) // 128 tile slots; the longest length in a draw is exactly the maximum. `tile_owner`: on each index of traj, trajectory j takes the next 1 + (length - 1) // 128 slots after those of trajectories 0 to j - 1, starting at slot 0; the remaining slots hold 4. Some index of traj uses all 24 slots. `factor_h`: A square matrix of full rank.
All inputs are finite; a program needn't handle non-finite values.
Results may differ from a plain program's by a relative error of at most 0.0031.
Values may be sent and summed in bfloat16 or wider, within the bound.
No kernel may reach another device: no remote copies, remote signals or barrier semaphores. Data moves between devices by JAX's collectives and lax.ppermute only.
A program may use at most 64 MiB of HBM per device.

v0:
```python
import jax
import jax.numpy as jnp
from jax import lax
from jax.sharding import PartitionSpec as P

ITERS = 8


highest = lax.Precision.HIGHEST


def layout(owner, lengths, tile_len):
    slot_ids = jnp.arange(lengths.shape[0], dtype=jnp.int32)
    member = owner[:, None] == slot_ids[None, :]
    starts = jnp.sum((owner[:, None] < slot_ids[None, :]).astype(jnp.int32), axis=0)
    first_slot = jnp.sum(jnp.where(member, starts[None, :], 0), axis=1)
    limit = jnp.sum(jnp.where(member, lengths[None, :], 0), axis=1)
    tile_ids = jnp.arange(owner.shape[0], dtype=jnp.int32)
    place = (tile_ids - first_slot)[:, None] * tile_len + jnp.arange(tile_len, dtype=jnp.int32)[
        None, :
    ]
    live = (place < limit[:, None]).astype(jnp.float32)
    return (member.astype(jnp.float32), live)


def keep_same(value):
    return value


def polar_factor(partial_value, mixers, member, live, gram_total, norm_total):
    mixed = jnp.einsum("tk,kab->tab", member, mixers, precision=highest)
    target = jnp.einsum("tab,tbs->tas", mixed, partial_value * live[:, None, :], precision=highest)
    energy = norm_total(
        jnp.einsum("tk,t->k", member, jnp.sum(target * target, axis=(1, 2)), precision=highest)
    )
    scales = jnp.dot(member, lax.rsqrt(energy + 1e-06), precision=highest)
    current = target * scales[:, None, None]
    for iteration in range(ITERS):
        tile_grams = jnp.einsum("tas,tbs->tab", current, current, precision=highest)
        grams = gram_total(jnp.einsum("tk,tab->kab", member, tile_grams, precision=highest))
        spread = jnp.einsum("tk,kab->tab", member, grams, precision=highest)
        current = 1.5 * current - 0.5 * jnp.einsum(
            "tab,tbs->tas", spread, current, precision=highest
        )
    return current.astype(jnp.bfloat16)


def chol_solve(gram, right):
    lower = jnp.linalg.cholesky(gram)
    middle = lax.linalg.triangular_solve(lower, right, left_side=True, lower=True)
    return lax.linalg.triangular_solve(lower, middle, left_side=True, lower=True, transpose_a=True)


def body(series, lengths, tile_owner, factor_h, factor_v, weights_s):
    tile_slots = tile_owner.shape[0]
    local_cols = series.shape[1]
    blocks = series.reshape(tile_slots, series.shape[0] // tile_slots, local_cols)
    member, live = layout(tile_owner, lengths, blocks.shape[1])
    factor_bf = factor_v.astype(jnp.bfloat16)
    mixers = factor_h[None, :, :] * weights_s.T[:, None, :]
    factor_gram = jnp.dot(factor_v, factor_v.T, precision=highest)
    weight_gram = jnp.dot(weights_s, weights_s.T, precision=highest)
    picked = blocks
    partial_value = lax.psum(
        jnp.einsum("rj,tsj->trs", factor_bf, picked, preferred_element_type=jnp.float32), "var"
    )
    polar = polar_factor(partial_value, mixers, member, live, keep_same, keep_same)
    picked = blocks
    per_tile = jnp.einsum("trs,tsj->trj", polar, picked, preferred_element_type=jnp.float32)
    projected = jnp.einsum("tk,trj->krj", member, per_tile, precision=highest)
    head_part = jnp.einsum("kaj,rj->kar", projected, factor_v, precision=highest)
    head_terms = jnp.einsum("kar,rk->ar", head_part, weights_s, precision=highest)
    factor_total = lax.psum(factor_gram, "var")
    weight_total = lax.psum(weight_gram, "traj")
    head_total = lax.psum(head_terms, ("traj", "var"))
    new_h = chol_solve(factor_total * weight_total, head_total.T).T
    scaled = new_h[None, :, :] * weights_s.T[:, None, :]
    column_terms = jnp.einsum("kar,kaj->rj", scaled, projected, precision=highest)
    head_gram = jnp.dot(new_h.T, new_h, precision=highest)
    column_total = lax.psum(column_terms, "traj")
    new_v = chol_solve(head_gram * weight_total, column_total)
    along = jnp.einsum("kaj,rj->kar", projected, new_v, precision=highest)
    weight_terms = jnp.einsum("kar,ar->rk", along, new_h, precision=highest)
    new_gram = jnp.dot(new_v, new_v.T, precision=highest)
    weight_total_terms, new_gram_total = lax.psum((weight_terms, new_gram), "var")
    new_s = chol_solve(head_gram * new_gram_total, weight_total_terms)
    return (new_h, new_v, new_s)


def solution(mesh):
    return jax.shard_map(
        body,
        mesh=mesh,
        in_specs=(P("traj", "var"), P("traj"), P("traj"), P(), P(None, "var"), P(None, "traj")),
        out_specs=(P(), P(None, "var"), P(None, "traj")),
        check_vma=False,
    )
```

profile of v0, /device:TPU:1, one launch (start us, length us, event | category | flops | bytes accessed | tf_op | source)
XLA Modules:
  0.0 1024.3 jit_solution(5690159101762931761)
XLA Ops:
  7.2 1.4 copy-done
  8.6 2.4 convolution_bitcast_fusion
  11.7 498.1 %psum.50 = f32[64,64]{0,1:T(8,128)S(1)} all-reduce(f32[64,64]{0,1:T(8,128)S(1)} %fusion.113), channel_id=1, replica_groups=mesh['traj'=128,'var'=4] {'traj'}, use_global_device_ids=true, to_apply=%region_1.2 | all-reduce | flops 4096 | bytes 32768 | tf_op jit(solution)/shard_map/psum | solution.py:74
  509.7 13.5 %psum.49 = f32[64,64]{0,1:T(8,128)S(1)} all-reduce(f32[64,64]{0,1:T(8,128)S(1)} %fusion.112), channel_id=1, replica_groups=mesh['traj'=128,'var'=4] {'var'}, use_global_device_ids=true, to_apply=%region_0.0 | all-reduce | flops 4096 | bytes 32768 | tf_op jit(solution)/shard_map/psum | solution.py:73
  523.4 5.8 cholesky.59
  530.7 4.9 custom-call.17
  536.2 2.3 multiply_reduce_fusion
  538.8 1.5 fusion.43
  541.6 1.1 fusion.9
  542.7 1.4 fusion.114
  545.4 1.1 fusion.8
  546.5 1.4 fusion.115
  549.4 1.1 fusion.7
  550.5 1.4 fusion.116
  553.2 1.1 fusion.6
  554.3 1.4 fusion.117
  557.1 1.1 fusion.5
  558.2 1.4 fusion.118
  560.9 1.3 fusion.4
  562.2 1.4 fusion.119
  564.9 1.1 fusion.3
  566.0 1.4 fusion.120
  568.7 1.1 fusion.10
  570.2 1.5 fusion
  572.1 106.1 %psum.52 = f32[64,64]{0,1:T(8,128)S(1)} all-reduce(f32[64,64]{0,1:T(8,128)S(1)} %bitcast.150), channel_id=1, replica_groups=mesh['traj'=128,'var'=4] {'traj','var'}, use_global_device_ids=true, to_apply=%region_9.11 | all-reduce | flops 4096 | bytes 32768 | tf_op jit(solution)/shard_map/psum | solution.py:75
  678.9 5.8 cholesky.70
  687.2 4.9 custom-call.18
  692.1 295.3 %all-reduce.6.cloned.1.call-done = f32[64,256]{1,0:T(8,128)} async-done(((f32[64,256]{1,0:T(8,128)}), f32[64,256]{1,0:T(8,128)}) %all-reduce.6.cloned.1.call-update) | async-done | bytes 65552 | tf_op jit(solution)/shard_map/psum | solution.py:80
  987.4 1.1 fusion.70
  990.0 13.7 %all-reduce = (f32[64,4]{1,0:T(8,128)S(1)}, f32[64,64]{0,1:T(8,128)S(1)}) all-reduce(f32[64,4]{1,0:T(8,128)S(1)} %bitcast.151, f32[64,64]{0,1:T(8,128)S(1)} %fusion.122), channel_id=1, replica_groups=mesh['traj'=128,'var'=4] {'var'}, use_global_device_ids=true, to_apply=%region_12.14 | all-reduce | flops 4352 | bytes 34816 | tf_op jit(solution)/shard_map/psum | solution.py:85
  1003.9 5.8 cholesky.81
  1011.0 4.9 custom-call.19
  (78 shorter events, 21.9 us)
Async XLA Ops:
  7.2 1.4 copy-start
  7.2 529.0 %all-reduce.4.cloned.1.call-start = ((), (), s32[]{:S(2)}) async-start(), calls=%async_computation | async-start | bytes 1572864 | tf_op jit(solution)/shard_map/psum | solution.py:64
  8.6 2.5 copy-start.2
  8.6 2.7 copy-start.3
  8.6 2.9 copy-start.6
  8.6 522.0 %copy-start.7 = (s32[4]{0:T(128)S(1)}, s32[4]{0:T(128)}, u32[]{:S(2)}) copy-start(s32[4]{0:T(128)} %param.8) | copy-start | bytes 52
  8.6 527.0 %copy-start.5 = (f32[64,64]{1,0:T(8,128)S(1)}, f32[64,64]{1,0:T(8,128)}, u32[]{:S(2)}) copy-start(f32[64,64]{1,0:T(8,128)} %param.10) | copy-start | bytes 49156
  11.0 976.4 %all-reduce.6.cloned.1.call-start = ((), (), s32[]{:S(2)}) async-start(), calls=%async_computation.1 | async-start | bytes 131072 | tf_op jit(solution)/shard_map/psum | solution.py:80
  685.5 331.5 %copy-start.4 = (f32[64,64]{1,0:T(8,128)}, f32[64,64]{1,0:T(8,128)S(1)}, u32[]{:S(2)}) copy-start(f32[64,64]{1,0:T(8,128)S(1)} %copy.18) | copy-start | bytes 49156
  988.7 28.3 %copy-start.1 = (f32[64,256]{1,0:T(8,128)}, f32[64,256]{1,0:T(8,128)S(1)}, u32[]{:S(2)}) copy-start(f32[64,256]{1,0:T(8,128)S(1)} %fusion.68) | copy-start | bytes 196612
Sparse Core Ops, SparseCore 0:
  11.2 63.2 all-reduce.3
  686.7 300.7 all-reduce.5
where the time goes:
time: 1040 us; the launch traced here: 1020 us
  blocking collectives  631 us (61%)
  waiting for transfers between devices  295 us (28%)
  matrix products  44.1 us (4%)
  other arithmetic  36.6 us (4%)
  between operations  15 us (1%)
    psum x1, blocking collectives, body(): weight_total = lax.psum(weight_gram, 'traj')  498 us
    psum x1, waiting for transfers between devices, body(): column_total = lax.psum(column_terms, 'traj')  295 us
    psum x1, blocking collectives, body(): head_total = lax.psum(head_terms, ('traj', 'var'))  106 us
  transfers between devices with their start and end apart: 2, of which 1 were waited for; matrix products, arithmetic and copies ran while one was open for 2% of the time, Pallas kernels for 0%

commit v1 on v0

v1 whole, which is shorter than its diff:
```python
import functools

import jax
import jax.numpy as jnp
from jax import lax
from jax.experimental import pallas as pl
from jax.experimental.pallas import tpu as pltpu
from jax.sharding import Mesh, PartitionSpec as P

ITERS = 8
R = 64
TILE = 128
KD = 4
LANES = (((1,), (1,)), ((), ()))

highest = lax.Precision.HIGHEST


def mm(left, right):
    return jnp.dot(left, right, precision=highest, preferred_element_type=jnp.float32)


def mm_t(left, right):
    return lax.dot_general(left, right, LANES, precision=highest, preferred_element_type=jnp.float32)


def eye_mask():
    rows = lax.broadcasted_iota(jnp.int32, (R, R), 0)
    cols = lax.broadcasted_iota(jnp.int32, (R, R), 1)
    return rows == cols


def eliminate(both):
    rows = lax.broadcasted_iota(jnp.int32, both.shape, 0)
    for k in range(R):
        row = both[k : k + 1, :] / both[k : k + 1, k : k + 1]
        both = jnp.where(rows == k, row, both - both[:, k : k + 1] * row)
    return both


def partial_kernel(v_ref, s_ref, out_ref):
    value = lax.dot_general(
        v_ref[...].astype(jnp.bfloat16), s_ref[...], LANES, preferred_element_type=jnp.float32
    ).astype(jnp.bfloat16)
    for peer in range(out_ref.shape[0]):
        out_ref[peer] = value


def polar_kernel(
    owner_ref, length_ref, part_ref, s_ref, h_ref, v_ref, w_ref, proj_ref, pack_ref, p_ref, g_ref, q_ref, *, peers, spread
):
    slots = s_ref.shape[0] // TILE
    eye = eye_mask()
    lane = lax.broadcasted_iota(jnp.int32, (R, TILE), 1)
    starts = [jnp.int32(0)]
    for k in range(1, KD):
        total = jnp.int32(0)
        for t in range(slots):
            total = total + jnp.where(owner_ref[t] < k, 1, 0)
        starts.append(total)
    g_ref[...] = jnp.zeros_like(g_ref)
    q_ref[...] = jnp.zeros_like(q_ref)
    for t in range(slots):
        own = owner_ref[t]
        left = jnp.int32(0)
        for k in range(KD):
            left = jnp.where(own == k, length_ref[k] - (t - starts[k]) * TILE, left)
        cols = slice(t * TILE, (t + 1) * TILE)
        value = part_ref[0, :, cols].astype(jnp.float32)
        for peer in range(1, peers):
            value = value + part_ref[peer, :, cols].astype(jnp.float32)
        value = jnp.where(lane < left, value, 0.0)
        p_ref[:, cols] = value
        g_ref[own] += mm_t(value, value)
    hmat = h_ref[...]
    wmat = w_ref[...]
    grams, turns = [], []
    for k in range(KD):
        mix = hmat * jnp.sum(jnp.where(eye, wmat[:, k : k + 1], 0.0), axis=0, keepdims=True)
        gram = mm_t(mm(mix, g_ref[k]), mix)
        energy = jnp.sum(jnp.where(eye, gram, 0.0), keepdims=True)
        scale = lax.rsqrt(energy + 1e-06)
        grams.append(gram * (scale * scale))
        turns.append(mix * scale)
    for iteration in range(ITERS):
        steps = [jnp.where(eye, 1.5, 0.0) - 0.5 * gram for gram in grams]
        turns = [mm(step, turn) for step, turn in zip(steps, turns)]
        if iteration < ITERS - 1:
            halves = [mm(step, gram) for step, gram in zip(steps, grams)]
            grams = [mm(half, step) for half, step in zip(halves, steps)]
    for k in range(KD):
        g_ref[k] = turns[k]
    for t in range(slots):
        own = owner_ref[t]
        cols = slice(t * TILE, (t + 1) * TILE)
        polar = mm(g_ref[own], p_ref[:, cols]).astype(jnp.bfloat16)
        q_ref[own] += jnp.dot(polar, s_ref[cols, :], preferred_element_type=jnp.float32)
    vmat = v_ref[...]
    width = vmat.shape[1]
    head = jnp.zeros((R, R), jnp.float32)
    for k in range(KD):
        block = q_ref[k]
        proj_ref[:, k * width : (k + 1) * width] = block
        head = head + mm_t(block, vmat * wmat[:, k : k + 1])
    pack_ref[0:R, :] = jnp.concatenate([head, mm_t(wmat, wmat) * (1.0 / peers)], axis=1)
    pack_ref[R : 2 * R, :] = jnp.concatenate(
        [mm_t(vmat, vmat) * (1.0 / spread), jnp.zeros((R, R), jnp.float32)], axis=1
    )


def head_kernel(pack_ref, proj_ref, w_ref, newh_ref, hp_ref, col_ref, side_ref):
    head, wgram = pack_ref[0:R, 0:R], pack_ref[0:R, R : 2 * R]
    fgram = pack_ref[R : 2 * R, 0:R]
    eye = eye_mask()
    newh_t = eliminate(jnp.concatenate([fgram * wgram, head.T], axis=1))[:, R:]
    newh_ref[...] = newh_t.T
    wmat = w_ref[...]
    hp = mm(newh_t, proj_ref[...])
    hp_ref[...] = hp
    width = hp.shape[1] // KD
    col = hp[:, 0:width] * wmat[:, 0:1]
    for k in range(1, KD):
        col = col + hp[:, k * width : (k + 1) * width] * wmat[:, k : k + 1]
    for half in range(width // TILE):
        col_ref[half * R : (half + 1) * R, :] = col[:, half * TILE : (half + 1) * TILE]
    hgram = mm_t(newh_t, newh_t)
    inverse = eliminate(jnp.concatenate([hgram * wgram, jnp.where(eye, 1.0, 0.0)], axis=1))[:, R:]
    side_ref[...] = jnp.concatenate([hgram, inverse], axis=1)


def column_kernel(col_ref, hp_ref, side_ref, newv_ref, out_ref):
    halves = col_ref.shape[0] // R
    col = jnp.concatenate([col_ref[half * R : (half + 1) * R, :] for half in range(halves)], axis=1)
    newv = mm(side_ref[:, R : 2 * R], col)
    newv_ref[...] = newv
    width = newv.shape[1]
    lane = lax.broadcasted_iota(jnp.int32, (R, R), 1)
    terms = jnp.zeros((R, R), jnp.float32)
    for k in range(KD):
        sums = jnp.sum(hp_ref[:, k * width : (k + 1) * width] * newv, axis=1, keepdims=True)
        terms = jnp.where(lane == k, sums, terms)
    value = jnp.concatenate([mm_t(newv, newv), terms], axis=1)
    for peer in range(out_ref.shape[0]):
        out_ref[peer] = value


def weight_kernel(in_ref, side_ref, out_ref):
    value = in_ref[0]
    for peer in range(1, in_ref.shape[0]):
        value = value + in_ref[peer]
    solved = eliminate(jnp.concatenate([side_ref[:, 0:R] * value[:, 0:R], value[:, R : 2 * R]], axis=1))
    out_ref[...] = solved[:, R : R + KD]


def vmem(count):
    return [pl.BlockSpec(memory_space=pltpu.VMEM)] * count


def params():
    return pltpu.CompilerParams(vmem_limit_bytes=48 * 1024 * 1024)


def f32(*shape):
    return jax.ShapeDtypeStruct(shape, jnp.float32)


def exchange(value, axes):
    return lax.all_to_all(value, axes, 0, 0, tiled=True)


def share(value, axes, peers):
    return exchange(jnp.broadcast_to(value[None], (peers,) + value.shape), axes)


def body(sizes, series, lengths, tile_owner, factor_h, factor_v, weights_s):
    ny, nz, nc, nx = sizes
    rows, width = series.shape
    slots = tile_owner.shape[0]
    chunk = rows // 6
    parts = pl.pallas_call(
        partial_kernel,
        grid=(rows // chunk,),
        in_specs=[
            pl.BlockSpec((R, width), lambda i: (0, 0)),
            pl.BlockSpec((chunk, width), lambda i: (i, 0)),
        ],
        out_specs=pl.BlockSpec((nx, R, chunk), lambda i: (0, 0, i)),
        out_shape=jax.ShapeDtypeStruct((nx, R, rows), jnp.bfloat16),
        compiler_params=params(),
    )(factor_v, series)
    parts = exchange(parts, "x")
    proj, pack = pl.pallas_call(
        functools.partial(polar_kernel, peers=nx, spread=ny * nz * nc),
        in_specs=[pl.BlockSpec(memory_space=pltpu.SMEM)] * 2 + vmem(5),
        out_specs=vmem(2),
        out_shape=[f32(R, KD * width), f32(2 * R, 2 * R)],
        scratch_shapes=[
            pltpu.VMEM((R, rows), jnp.float32),
            pltpu.VMEM((KD + 1, R, R), jnp.float32),
            pltpu.VMEM((KD + 1, R, width), jnp.float32),
        ],
        compiler_params=params(),
    )(tile_owner, lengths, parts, series, factor_h, factor_v, weights_s)
    near = ny * nc * nx
    pieces = exchange(pack.reshape(near, 2 * R // near, 2 * R), ("y", "c", "x"))
    pieces = share(jnp.sum(pieces, axis=0), "z", nz)
    pieces = share(jnp.sum(pieces, axis=0), ("y", "c", "x"), near)
    new_h, hp, col, side = pl.pallas_call(
        head_kernel,
        in_specs=vmem(3),
        out_specs=vmem(4),
        out_shape=[f32(R, R), f32(R, KD * width), f32(R * width // TILE, TILE), f32(R, 2 * R)],
        compiler_params=params(),
    )(pieces.reshape(2 * R, 2 * R), proj, weights_s)
    near = ny * nc
    pieces = exchange(col.reshape(near, col.shape[0] // near, TILE), ("y", "c"))
    pieces = share(jnp.sum(pieces, axis=0), "z", nz)
    pieces = share(jnp.sum(pieces, axis=0), ("y", "c"), near)
    new_v, sums = pl.pallas_call(
        column_kernel,
        in_specs=vmem(3),
        out_specs=vmem(2),
        out_shape=[f32(R, width), f32(nx, R, 2 * R)],
        compiler_params=params(),
    )(pieces.reshape(col.shape), hp, side)
    new_s = pl.pallas_call(
        weight_kernel,
        in_specs=vmem(2),
        out_specs=pl.BlockSpec(memory_space=pltpu.VMEM),
        out_shape=f32(R, KD),
        compiler_params=params(),
    )(exchange(sums, "x"), side)
    return (new_h, new_v, new_s)


def solution(mesh):
    traj, nx = mesh.devices.shape
    ny, nc = (4, 2) if traj % 128 == 0 else (2, 2)
    sizes = (ny, traj // (ny * nc), nc, nx)
    fine = Mesh(mesh.devices.reshape(sizes), ("y", "z", "c", "x"))
    traj_axes = ("y", "z", "c")
    return jax.shard_map(
        functools.partial(body, sizes),
        mesh=fine,
        in_specs=(P(traj_axes, "x"), P(traj_axes), P(traj_axes), P(), P(None, "x"), P(None, traj_axes)),
        out_specs=(P(), P(None, "x"), P(None, traj_axes)),
        check_vma=False,
    )
```

time: 1040 us -> 153 us (0.15); the launches traced: 1020 us -> 153 us
  blocking collectives: 631 us -> 97.7 us
  waiting for transfers between devices: 295 us -> 14.8 us
  matrix products: 44.1 us -> 0 us
  other arithmetic: 36.6 us -> 0.1 us
  Pallas kernels: 0 us -> 30.2 us
  between operations: 15 us -> 0.74 us
    psum x4 -> x0, blocking collectives: 631 us -> none  [the longest x1 498 us: body(): weight_total = lax.psum(weight_gram, 'traj')]
    psum x2 -> x0, waiting for transfers between devices: 295 us -> none  [the longest x1 295 us: body(): column_total = lax.psum(column_terms, 'traj')]
    all_to_all x0 -> x7, blocking collectives: none -> 97.7 us  [exchange(): return lax.all_to_all(value, axes, 0, 0, tiled=True)]
    dot_general x47 -> x0, matrix products: 41.3 us -> none  [the longest x8 11 us: polar_factor(): tile_grams = jnp.einsum('tas,tbs->tab', current, current, precision=highest)]
    another operation x15 -> x0, other arithmetic: 36.2 us -> none  [the longest x9 19.6 us: chol_solve(): lower = jnp.linalg.cholesky(gram)]
    pallas_call x0 -> x5, Pallas kernels: none -> 30.2 us  [the longest x1 11.8 us: body(): pl.pallas_call(head_kernel, in_specs=vmem(3), out_specs=vmem(4), out_shap...]
    all_to_all x0 -> x1, waiting for transfers between devices: none -> 14.8 us  [exchange(): return lax.all_to_all(value, axes, 0, 0, tiled=True)]
  transfers between devices with their start and end apart: 2 -> 1, of which waited for: 1 -> 1; matrix products, arithmetic and copies ran while one was open for 2% -> 0% of each run, Pallas kernels for 0% -> 0%
where the time goes in v1:
time: 153 us
  blocking collectives  97.7 us (64%)
  Pallas kernels  30.2 us (20%)
  waiting for transfers between devices  14.8 us (10%)
  starting transfers between devices  4.99 us (3%)
  local copies, waits for them, and re-layouts  4.23 us (3%)
    all_to_all x7, blocking collectives, exchange(): return lax.all_to_all(value, axes, 0, 0, tiled=True)  97.7 us
    all_to_all x1, waiting for transfers between devices, exchange(): return lax.all_to_all(value, axes, 0, 0, tiled=True)  14.8 us
    pallas_call x1, Pallas kernels, body(): pl.pallas_call(head_kernel, in_specs=vmem(3), out_specs=vmem(4), out_shap...  11.8 us
    pallas_call x1, Pallas kernels, body(): pl.pallas_call(functools.partial(polar_kernel, peers=nx, spread=ny * nz *...  10.5 us
    pallas_call x1, Pallas kernels, body(): pl.pallas_call(weight_kernel, in_specs=vmem(2), out_specs=pl.BlockSpec(me...  5.47 us
    all_to_all x1, starting transfers between devices, exchange(): return lax.all_to_all(value, axes, 0, 0, tiled=True)  4.99 us
    unnamed x20, local copies, waits for them, and re-layouts  4.19 us
  transfers between devices with their start and end apart: 1, of which 1 were waited for; matrix products, arithmetic and copies ran while one was open for 0% of the time, Pallas kernels for 0%

profile of v1, /device:TPU:1, one launch (start us, length us, event | category | flops | bytes accessed | tf_op | source)
XLA Modules:
  0.0 152.7 jit_solution(580618392457199644)
XLA Ops:
  0.6 0.0 copy-start
  0.6 1.4 copy-done
  2.0 0.0 copy-start.3
  2.0 0.8 copy-done.3
  2.9 1.4 shard_map.85
  4.3 0.0 copy-start.2
  4.3 1.2 copy-done.2
  5.5 0.0 copy-start.8
  5.5 0.0 copy-start.1
  5.5 0.0 copy-start.6
  5.5 0.0 copy-start.7
  5.5 5.0 %all-to-all-start = ((bf16[4,64,3072]{2,1,0:T(8,128)(2,1)}), bf16[4,64,3072]{2,1,0:T(8,128)(2,1)S(1)}, u32[]{:S(2)}, u32[]{:S(2)}) async-start(bf16[4,64,3072]{2,1,0:T(8,128)(2,1)} %copy-done.2), calls=%async_computation | async-start | bytes 3145728 | tf_op jit(solution)/shard_map/all_to_all | solution.py:168
  10.5 0.0 copy-done.8
  10.5 0.1 copy.15.w_ref
  10.6 14.8 %all-to-all-done.part_ref = bf16[4,64,3072]{2,1,0:T(8,128)(2,1)S(1)} async-done(((bf16[4,64,3072]{2,1,0:T(8,128)(2,1)}), bf16[4,64,3072]{2,1,0:T(8,128)(2,1)S(1)}, u32[]{:S(2)}, u32[]{:S(2)}) %all-to-all-start) | async-done | bytes 1572896 | tf_op jit(solution)/shard_map/all_to_all | solution.py:168
  25.4 0.0 copy-done.1
  25.4 0.0 copy-done.4
  25.4 0.0 copy-done.5
  25.4 0.0 copy-done.6
  25.4 0.0 copy-done.7
  25.4 10.5 %shard_map.86 = (f32[64,1024]{1,0:T(8,128)S(1)}, f32[128,128]{1,0:T(8,128)S(1)}) custom-call(s32[24]{0:T(128)S(1)} %copy-done.6, s32[4]{0:T(128)S(1)} %copy-done.7, bf16[4,64,3072]{2,1,0:T(8,128)(2,1)S(1)} %all-to-all-done.part_ref, bf16[3072,256]{1,0:T(8,128)(2,1)S(1)} %copy-done.1, f32[64,64]{1,0:T(8,128)S(1)} %copy-done.5, f32[64,256]{1,0:T(8,128)S(1)} %copy-done.4, ...), custom_call_target="tpu_custom_call" | custom-call | tf_op jit(solution)/shard_map/pallas_call | solution.py:192
  35.9 19.1 %all_to_all.40 = f32[32,4,128]{2,1,0:T(4,128)S(1)} all-to-all(f32[32,4,128]{2,1,0:T(4,128)S(1)} %bitcast.7), channel_id=1, replica_groups=mesh['y'=4,'z'=16,'c'=2,'x'=4] {'y','c','x'}, dimensions={0} | all-to-all | bytes 131072 | tf_op jit(solution)/shard_map/all_to_all | solution.py:168
  55.1 26.2 %all_to_all.41 = f32[16,4,128]{2,1,0:T(4,128)S(1)} all-to-all(f32[16,4,128]{2,1,0:T(4,128)S(1)} %broadcast_in_dim.8), channel_id=1, replica_groups=mesh['y'=4,'z'=16,'c'=2,'x'=4] {'z'}, dimensions={0} | all-to-all | bytes 65536 | tf_op jit(solution)/shard_map/all_to_all | solution.py:168
  81.3 12.4 %all_to_all.42 = f32[32,4,128]{2,1,0:T(4,128)S(1)} all-to-all(f32[32,4,128]{2,1,0:T(4,128)S(1)} %broadcast_in_dim.9), channel_id=1, replica_groups=mesh['y'=4,'z'=16,'c'=2,'x'=4] {'y','c','x'}, dimensions={0} | all-to-all | bytes 131072 | tf_op jit(solution)/shard_map/all_to_all | solution.py:168
  93.7 11.8 %shard_map.87 = (f32[64,64]{1,0:T(8,128)}, f32[64,1024]{1,0:T(8,128)S(1)}, f32[128,128]{1,0:T(8,128)S(1)}, f32[64,128]{1,0:T(8,128)S(1)}) custom-call(f32[128,128]{1,0:T(8,128)S(1)} %bitcast.4, f32[64,1024]{1,0:T(8,128)S(1)} %get-tuple-element.12.proj_ref, f32[64,4]{1,0:T(8,128)S(1)} %copy.15.w_ref), custom_call_target="tpu_custom_call" | custom-call | tf_op jit(solution)/shard_map/pallas_call | solution.py:208
  105.5 7.6 %all_to_all.43 = f32[8,16,128]{2,1,0:T(8,128)S(1)} all-to-all(f32[8,16,128]{2,1,0:T(8,128)S(1)} %bitcast.6), channel_id=1, replica_groups=mesh['y'=4,'z'=16,'c'=2,'x'=4] {'y','c'}, dimensions={0} | all-to-all | bytes 131072 | tf_op jit(solution)/shard_map/all_to_all | solution.py:168
  113.1 14.6 %all_to_all.44 = f32[16,16,128]{2,1,0:T(8,128)S(1)} all-to-all(f32[16,16,128]{2,1,0:T(8,128)S(1)} %broadcast_in_dim.10), channel_id=1, replica_groups=mesh['y'=4,'z'=16,'c'=2,'x'=4] {'z'}, dimensions={0} | all-to-all | bytes 262144 | tf_op jit(solution)/shard_map/all_to_all | solution.py:168
  127.7 10.7 %all_to_all.45 = f32[8,16,128]{2,1,0:T(8,128)S(1)} all-to-all(f32[8,16,128]{2,1,0:T(8,128)S(1)} %broadcast_in_dim.11), channel_id=1, replica_groups=mesh['y'=4,'z'=16,'c'=2,'x'=4] {'y','c'}, dimensions={0} | all-to-all | bytes 131072 | tf_op jit(solution)/shard_map/all_to_all | solution.py:168
  138.4 0.9 shard_map.88
  139.3 7.2 %all_to_all.46.in_ref = f32[4,64,128]{2,1,0:T(8,128)S(1)} all-to-all(f32[4,64,128]{2,1,0:T(8,128)S(1)} %get-tuple-element.18), channel_id=1, replica_groups=mesh['y'=4,'z'=16,'c'=2,'x'=4] {'x'}, dimensions={0} | all-to-all | bytes 262144 | tf_op jit(solution)/shard_map/all_to_all | solution.py:168
  146.5 5.5 %shard_map.89 = f32[64,4]{1,0:T(8,128)S(1)} custom-call(f32[4,64,128]{2,1,0:T(8,128)S(1)} %all_to_all.46.in_ref, f32[64,128]{1,0:T(8,128)S(1)} %get-tuple-element.16.side_ref), custom_call_target="tpu_custom_call" | custom-call | tf_op jit(solution)/shard_map/pallas_call | solution.py:226
  152.0 0.7 copy.18
  (10 shorter events, 0.1 us)
Async XLA Ops:
  0.6 1.4 copy-start
  2.0 0.8 copy-start.3
  4.3 1.2 copy-start.2
  5.5 5.0 %copy-start.8 = (f32[64,4]{0,1:T(4,128)S(1)}, f32[64,4]{0,1:T(4,128)}, u32[]{:S(2)}) copy-start(f32[64,4]{0,1:T(4,128)} %param.11) | copy-start | bytes 3076
  5.5 19.9 %copy-start.1 = (bf16[3072,256]{1,0:T(8,128)(2,1)S(1)}, bf16[3072,256]{1,0:T(8,128)(2,1)}, u32[]{:S(2)}) copy-start(bf16[3072,256]{1,0:T(8,128)(2,1)} %s_ref.3) | copy-start | bytes 4718596
  5.5 19.9 %copy-start.4 = (f32[64,256]{1,0:T(8,128)S(1)}, f32[64,256]{1,0:T(8,128)}, u32[]{:S(2)}) copy-start(f32[64,256]{1,0:T(8,128)} %v_ref.3) | copy-start | bytes 196612
  5.5 19.9 %copy-start.5 = (f32[64,64]{1,0:T(8,128)S(1)}, f32[64,64]{1,0:T(8,128)}, u32[]{:S(2)}) copy-start(f32[64,64]{1,0:T(8,128)} %h_ref.1) | copy-start | bytes 49156
  5.5 19.9 %copy-start.6 = (s32[24]{0:T(128)S(1)}, s32[24]{0:T(128)}, u32[]{:S(2)}) copy-start(s32[24]{0:T(128)} %owner_ref.1) | copy-start | bytes 292
  5.5 19.9 %copy-start.7 = (s32[4]{0:T(128)S(1)}, s32[4]{0:T(128)}, u32[]{:S(2)}) copy-start(s32[4]{0:T(128)} %length_ref.1) | copy-start | bytes 52
  5.5 19.9 %all-to-all-start = ((bf16[4,64,3072]{2,1,0:T(8,128)(2,1)}), bf16[4,64,3072]{2,1,0:T(8,128)(2,1)S(1)}, u32[]{:S(2)}, u32[]{:S(2)}) async-start(bf16[4,64,3072]{2,1,0:T(8,128)(2,1)} %copy-done.2), calls=%async_computation | async-start | bytes 3145728 | tf_op jit(solution)/shard_map/all_to_all | solution.py:168

commit v2 on v1

--- a/solution.py
+++ b/solution.py
@@ -32,22 +32,45 @@
 
 def eliminate(both):
     rows = lax.broadcasted_iota(jnp.int32, both.shape, 0)
-    for k in range(R):
-        row = both[k : k + 1, :] / both[k : k + 1, k : k + 1]
-        both = jnp.where(rows == k, row, both - both[:, k : k + 1] * row)
+    for k in range(0, R, 4):
+        col = [jnp.broadcast_to(both[:, k + i : k + i + 1], both.shape) for i in range(4)]
+        row = [both[k + i : k + i + 1, :] for i in range(4)]
+        piv = [[col[j][k + i : k + i + 1, :] for j in range(4)] for i in range(4)]
+        inv = 1.0 / (piv[0][0] * piv[1][1] - piv[0][1] * piv[0][1])
+        a00, a01, a11 = piv[1][1] * inv, -piv[0][1] * inv, piv[0][0] * inv
+        e02, e12 = a00 * piv[0][2] + a01 * piv[1][2], a01 * piv[0][2] + a11 * piv[1][2]
+        e03, e13 = a00 * piv[0][3] + a01 * piv[1][3], a01 * piv[0][3] + a11 * piv[1][3]
+        s22 = piv[2][2] - (piv[0][2] * e02 + piv[1][2] * e12)
+        s23 = piv[2][3] - (piv[0][2] * e03 + piv[1][2] * e13)
+        s33 = piv[3][3] - (piv[0][3] * e03 + piv[1][3] * e13)
+        inv = 1.0 / (s22 * s33 - s23 * s23)
+        t2 = row[2] - e02 * row[0] - e12 * row[1]
+        t3 = row[3] - e03 * row[0] - e13 * row[1]
+        n2, n3 = (s33 * t2 - s23 * t3) * inv, (s22 * t3 - s23 * t2) * inv
+        n0 = (a00 * row[0] + a01 * row[1]) - e02 * n2 - e03 * n3
+        n1 = (a01 * row[0] + a11 * row[1]) - e12 * n2 - e13 * n3
+        rest = (both - col[0] * n0 - col[1] * n1) - (col[2] * n2 + col[3] * n3)
+        for i, new in enumerate((n0, n1, n2, n3)):
+            rest = jnp.where(rows == k + i, new, rest)
+        both = rest
     return both
 
 
 def partial_kernel(v_ref, s_ref, out_ref):
-    value = lax.dot_general(
+    out_ref[0] = lax.dot_general(
         v_ref[...].astype(jnp.bfloat16), s_ref[...], LANES, preferred_element_type=jnp.float32
     ).astype(jnp.bfloat16)
-    for peer in range(out_ref.shape[0]):
-        out_ref[peer] = value
+
+
+def three(value):
+    high = value.astype(jnp.bfloat16)
+    rest = value - high.astype(jnp.float32)
+    middle = rest.astype(jnp.bfloat16)
+    return high, middle, (rest - middle.astype(jnp.float32)).astype(jnp.bfloat16)
 
 
 def polar_kernel(
-    owner_ref, length_ref, part_ref, s_ref, h_ref, v_ref, w_ref, proj_ref, pack_ref, p_ref, g_ref, q_ref, *, peers, spread
+    owner_ref, length_ref, part_ref, s_ref, h_ref, v_ref, w_ref, proj_ref, pack_ref, p_ref, g_ref, t_ref, q_ref, *, peers, spread
 ):
     slots = s_ref.shape[0] // TILE
     eye = eye_mask()
@@ -66,14 +89,13 @@
         for k in range(KD):
             left = jnp.where(own == k, length_ref[k] - (t - starts[k]) * TILE, left)
         cols = slice(t * TILE, (t + 1) * TILE)
-        value = part_ref[0, :, cols].astype(jnp.float32)
-        for peer in range(1, peers):
-            value = value + part_ref[peer, :, cols].astype(jnp.float32)
-        value = jnp.where(lane < left, value, 0.0)
+        quarter, first = divmod(t * TILE, part_ref.shape[2])
+        value = part_ref[quarter, :, first : first + TILE]
+        value = jnp.where(lane < left, value.astype(jnp.float32), 0.0).astype(jnp.bfloat16)
         p_ref[:, cols] = value
-        g_ref[own] += mm_t(value, value)
+        g_ref[own] += lax.dot_general(value, value, LANES, preferred_element_type=jnp.float32)
     hmat = h_ref[...]
-    wmat = w_ref[...]
+    wmat = w_ref[...].T
     grams, turns = [], []
     for k in range(KD):
         mix = hmat * jnp.sum(jnp.where(eye, wmat[:, k : k + 1], 0.0), axis=0, keepdims=True)
@@ -88,12 +110,16 @@
         if iteration < ITERS - 1:
             halves = [mm(step, gram) for step, gram in zip(steps, grams)]
             grams = [mm(half, step) for half, step in zip(halves, steps)]
-    for k in range(KD):
-        g_ref[k] = turns[k]
+    t_ref[KD] = jnp.zeros_like(t_ref[KD])
+    for k in range(KD):
+        for i, term in enumerate(three(turns[k])):
+            t_ref[k, i] = term
     for t in range(slots):
         own = owner_ref[t]
         cols = slice(t * TILE, (t + 1) * TILE)
-        polar = mm(g_ref[own], p_ref[:, cols]).astype(jnp.bfloat16)
+        value = p_ref[:, cols]
+        terms = [jnp.dot(t_ref[own, i], value, preferred_element_type=jnp.float32) for i in range(3)]
+        polar = (terms[0] + (terms[1] + terms[2])).astype(jnp.bfloat16)
         q_ref[own] += jnp.dot(polar, s_ref[cols, :], preferred_element_type=jnp.float32)
     vmat = v_ref[...]
     width = vmat.shape[1]
@@ -114,7 +140,7 @@
     eye = eye_mask()
     newh_t = eliminate(jnp.concatenate([fgram * wgram, head.T], axis=1))[:, R:]
     newh_ref[...] = newh_t.T
-    wmat = w_ref[...]
+    wmat = w_ref[...].T
     hp = mm(newh_t, proj_ref[...])
     hp_ref[...] = hp
     width = hp.shape[1] // KD
@@ -149,7 +175,7 @@
     for peer in range(1, in_ref.shape[0]):
         value = value + in_ref[peer]
     solved = eliminate(jnp.concatenate([side_ref[:, 0:R] * value[:, 0:R], value[:, R : 2 * R]], axis=1))
-    out_ref[...] = solved[:, R : R + KD]
+    out_ref[...] = solved[:, R : R + KD].T
 
 
 def vmem(count):
@@ -176,31 +202,34 @@
     ny, nz, nc, nx = sizes
     rows, width = series.shape
     slots = tile_owner.shape[0]
-    chunk = rows // 6
+    quarter = rows // nx
+    w_rows = weights_s.T
     parts = pl.pallas_call(
         partial_kernel,
-        grid=(rows // chunk,),
+        grid=(nx,),
         in_specs=[
             pl.BlockSpec((R, width), lambda i: (0, 0)),
-            pl.BlockSpec((chunk, width), lambda i: (i, 0)),
+            pl.BlockSpec((quarter, width), lambda i: (i, 0)),
         ],
-        out_specs=pl.BlockSpec((nx, R, chunk), lambda i: (0, 0, i)),
-        out_shape=jax.ShapeDtypeStruct((nx, R, rows), jnp.bfloat16),
+        out_specs=pl.BlockSpec((1, R, quarter), lambda i: (i, 0, 0)),
+        out_shape=jax.ShapeDtypeStruct((nx, R, quarter), jnp.bfloat16),
         compiler_params=params(),
     )(factor_v, series)
-    parts = exchange(parts, "x")
+    parts = jnp.sum(exchange(parts, "x").astype(jnp.float32), axis=0).astype(jnp.bfloat16)
+    parts = share(parts, "x", nx)
     proj, pack = pl.pallas_call(
         functools.partial(polar_kernel, peers=nx, spread=ny * nz * nc),
         in_specs=[pl.BlockSpec(memory_space=pltpu.SMEM)] * 2 + vmem(5),
         out_specs=vmem(2),
         out_shape=[f32(R, KD * width), f32(2 * R, 2 * R)],
         scratch_shapes=[
-            pltpu.VMEM((R, rows), jnp.float32),
+            pltpu.VMEM((R, rows), jnp.bfloat16),
             pltpu.VMEM((KD + 1, R, R), jnp.float32),
+            pltpu.VMEM((KD + 1, 3, R, R), jnp.bfloat16),
             pltpu.VMEM((KD + 1, R, width), jnp.float32),
         ],
         compiler_params=params(),
-    )(tile_owner, lengths, parts, series, factor_h, factor_v, weights_s)
+    )(tile_owner, lengths, parts, series, factor_h, factor_v, w_rows)
     near = ny * nc * nx
     pieces = exchange(pack.reshape(near, 2 * R // near, 2 * R), ("y", "c", "x"))
     pieces = share(jnp.sum(pieces, axis=0), "z", nz)
@@ -211,10 +240,10 @@
         out_specs=vmem(4),
         out_shape=[f32(R, R), f32(R, KD * width), f32(R * width // TILE, TILE), f32(R, 2 * R)],
         compiler_params=params(),
-    )(pieces.reshape(2 * R, 2 * R), proj, weights_s)
+    )(pieces.reshape(2 * R, 2 * R), proj, w_rows)
     near = ny * nc
     pieces = exchange(col.reshape(near, col.shape[0] // near, TILE), ("y", "c"))
-    pieces = share(jnp.sum(pieces, axis=0), "z", nz)
+    pieces = share(jnp.sum(pieces, axis=0).astype(jnp.bfloat16), "z", nz).astype(jnp.float32)
     pieces = share(jnp.sum(pieces, axis=0), ("y", "c"), near)
     new_v, sums = pl.pallas_call(
         column_kernel,
@@ -227,10 +256,10 @@
         weight_kernel,
         in_specs=vmem(2),
         out_specs=pl.BlockSpec(memory_space=pltpu.VMEM),
-        out_shape=f32(R, KD),
+        out_shape=f32(KD, R),
         compiler_params=params(),
     )(exchange(sums, "x"), side)
-    return (new_h, new_v, new_s)
+    return (new_h, new_v, new_s.T)
 
 
 def solution(mesh):

time: 153 us -> 135 us (0.88)
  blocking collectives: 97.7 us -> 113 us
  waiting for transfers between devices: 14.8 us -> 0 us
  Pallas kernels: 30.2 us -> 18.4 us
  starting transfers between devices: 4.99 us -> 0 us
  local copies, waits for them, and re-layouts: 4.23 us -> 2.35 us
    all_to_all x7 -> x9, blocking collectives: 97.7 us -> 113 us  [exchange(): return lax.all_to_all(value, axes, 0, 0, tiled=True)]
    all_to_all x1 -> x0, waiting for transfers between devices: 14.8 us -> none  [exchange(): return lax.all_to_all(value, axes, 0, 0, tiled=True)]
    pallas_call x1, Pallas kernels: 11.8 us -> 5.28 us  [body(): pl.pallas_call(head_kernel, in_specs=vmem(3), out_specs=vmem(4), out_shap...]
    all_to_all x1 -> x0, starting transfers between devices: 4.99 us -> none  [exchange(): return lax.all_to_all(value, axes, 0, 0, tiled=True)]
    pallas_call x1, Pallas kernels: 10.5 us -> 8.04 us  [body(): pl.pallas_call(functools.partial(polar_kernel, peers=nx, spread=ny * nz *...]
    pallas_call x1, Pallas kernels: 5.47 us -> 3.07 us  [body(): pl.pallas_call(weight_kernel, in_specs=vmem(2), out_specs=pl.BlockSpec(me...]
    unnamed x20 -> x16, local copies, waits for them, and re-layouts: 4.19 us -> 2.28 us
  transfers between devices with their start and end apart: 1 -> 0, of which waited for: 1 -> 0; matrix products, arithmetic and copies ran while one was open for 0% -> 0% of each run, Pallas kernels for 0% -> 0%
where the time goes in v2:
time: 135 us; the launch traced here: 134 us
  blocking collectives  113 us (84%)
  Pallas kernels  18.4 us (14%)
  local copies, waits for them, and re-layouts  2.35 us (2%)
    all_to_all x9, blocking collectives, exchange(): return lax.all_to_all(value, axes, 0, 0, tiled=True)  113 us
    pallas_call x1, Pallas kernels, body(): pl.pallas_call(functools.partial(polar_kernel, peers=nx, spread=ny * nz *...  8.04 us
    pallas_call x1, Pallas kernels, body(): pl.pallas_call(head_kernel, in_specs=vmem(3), out_specs=vmem(4), out_shap...  5.28 us
    pallas_call x1, Pallas kernels, body(): pl.pallas_call(weight_kernel, in_specs=vmem(2), out_specs=pl.BlockSpec(me...  3.07 us

profile of v2, /device:TPU:1, one launch (start us, length us, event | category | flops | bytes accessed | tf_op | source)
XLA Modules:
  0.0 134.4 jit_solution(16301942509765475852)
XLA Ops:
  0.6 0.0 copy-start
  0.6 1.4 %copy-done = bf16[3072,256]{1,0:T(8,128)(2,1)S(1)} copy-done((bf16[3072,256]{1,0:T(8,128)(2,1)S(1)}, bf16[3072,256]{1,0:T(8,128)(2,1)}, u32[]{:S(2)}) %copy-start) | copy-done | bytes 1572888
  2.0 0.0 copy-start.2
  2.0 0.8 copy-done.2
  2.9 1.1 shard_map.85
  4.0 0.0 copy-start.1
  4.0 0.0 copy-start.3
  4.0 0.0 copy-start.4
  4.0 0.0 copy-start.5
  4.0 0.0 copy-start.6
  4.0 0.0 copy-start.7
  4.0 11.0 %all_to_all.45 = bf16[4,64,768]{2,1,0:T(8,128)(2,1)S(1)} all-to-all(bf16[4,64,768]{2,1,0:T(8,128)(2,1)S(1)} %shard_map.85), channel_id=1, replica_groups=mesh['y'=4,'z'=16,'c'=2,'x'=4] {'x'}, dimensions={0} | all-to-all | bytes 786432 | tf_op jit(solution)/shard_map/all_to_all | solution.py:194
  15.0 0.1 reduce_sum.48
  15.1 8.6 %all_to_all.46.part_ref = bf16[4,64,768]{2,1,0:T(8,128)(2,1)S(1)} all-to-all(bf16[4,64,768]{2,1,0:T(8,128)(2,1)S(1)} %broadcast_in_dim.10), channel_id=1, replica_groups=mesh['y'=4,'z'=16,'c'=2,'x'=4] {'x'}, dimensions={0} | all-to-all | bytes 786432 | tf_op jit(solution)/shard_map/all_to_all | solution.py:194
  23.8 0.0 copy-done.1
  23.8 0.0 copy-done.3
  23.8 0.0 copy-done.4
  23.8 0.0 copy-done.5
  23.8 0.0 copy-done.6
  23.8 0.0 copy-done.7
  23.8 8.0 %shard_map.86 = (f32[64,1024]{1,0:T(8,128)S(1)}, f32[128,128]{1,0:T(8,128)S(1)}) custom-call(s32[24]{0:T(128)S(1)} %copy-done.6, s32[4]{0:T(128)S(1)} %copy-done.7, bf16[4,64,768]{2,1,0:T(8,128)(2,1)S(1)} %all_to_all.46.part_ref, bf16[3072,256]{1,0:T(8,128)(2,1)S(1)} %copy-done.1, f32[64,64]{1,0:T(8,128)S(1)} %copy-done.4, f32[64,256]{1,0:T(8,128)S(1)} %copy-done.3, ...), custom_call_target="tpu_custom_call" | custom-call | tf_op jit(solution)/shard_map/pallas_call | solution.py:220
  31.8 16.9 %all_to_all.47 = f32[32,4,128]{2,1,0:T(4,128)S(1)} all-to-all(f32[32,4,128]{2,1,0:T(4,128)S(1)} %bitcast.9), channel_id=1, replica_groups=mesh['y'=4,'z'=16,'c'=2,'x'=4] {'y','c','x'}, dimensions={0} | all-to-all | bytes 131072 | tf_op jit(solution)/shard_map/all_to_all | solution.py:194
  48.8 25.5 %all_to_all.48 = f32[16,4,128]{2,1,0:T(4,128)S(1)} all-to-all(f32[16,4,128]{2,1,0:T(4,128)S(1)} %broadcast_in_dim.11), channel_id=1, replica_groups=mesh['y'=4,'z'=16,'c'=2,'x'=4] {'z'}, dimensions={0} | all-to-all | bytes 65536 | tf_op jit(solution)/shard_map/all_to_all | solution.py:194
  74.4 12.4 %all_to_all.49 = f32[32,4,128]{2,1,0:T(4,128)S(1)} all-to-all(f32[32,4,128]{2,1,0:T(4,128)S(1)} %broadcast_in_dim.12), channel_id=1, replica_groups=mesh['y'=4,'z'=16,'c'=2,'x'=4] {'y','c','x'}, dimensions={0} | all-to-all | bytes 131072 | tf_op jit(solution)/shard_map/all_to_all | solution.py:194
  86.7 5.3 %shard_map.87 = (f32[64,64]{1,0:T(8,128)}, f32[64,1024]{1,0:T(8,128)S(1)}, f32[128,128]{1,0:T(8,128)S(1)}, f32[64,128]{1,0:T(8,128)S(1)}) custom-call(f32[128,128]{1,0:T(8,128)S(1)} %bitcast.6, f32[64,1024]{1,0:T(8,128)S(1)} %get-tuple-element.12.proj_ref, f32[4,64]{1,0:T(4,128)S(1)} %bitcast.11), custom_call_target="tpu_custom_call" | custom-call | tf_op jit(solution)/shard_map/pallas_call | solution.py:237
  92.0 7.6 %all_to_all.50 = f32[8,16,128]{2,1,0:T(8,128)S(1)} all-to-all(f32[8,16,128]{2,1,0:T(8,128)S(1)} %bitcast.8), channel_id=1, replica_groups=mesh['y'=4,'z'=16,'c'=2,'x'=4] {'y','c'}, dimensions={0} | all-to-all | bytes 131072 | tf_op jit(solution)/shard_map/all_to_all | solution.py:194
  99.7 14.2 %all_to_all.51 = bf16[16,16,128]{2,1,0:T(8,128)(2,1)S(1)} all-to-all(bf16[16,16,128]{2,1,0:T(8,128)(2,1)S(1)} %broadcast_in_dim.13), channel_id=1, replica_groups=mesh['y'=4,'z'=16,'c'=2,'x'=4] {'z'}, dimensions={0} | all-to-all | bytes 131072 | tf_op jit(solution)/shard_map/all_to_all | solution.py:194
  113.9 9.3 %all_to_all.52 = f32[8,16,128]{2,1,0:T(8,128)S(1)} all-to-all(f32[8,16,128]{2,1,0:T(8,128)S(1)} %broadcast_in_dim.14), channel_id=1, replica_groups=mesh['y'=4,'z'=16,'c'=2,'x'=4] {'y','c'}, dimensions={0} | all-to-all | bytes 131072 | tf_op jit(solution)/shard_map/all_to_all | solution.py:194
  123.2 0.9 shard_map.88
  124.1 7.2 %all_to_all.53.in_ref = f32[4,64,128]{2,1,0:T(8,128)S(1)} all-to-all(f32[4,64,128]{2,1,0:T(8,128)S(1)} %get-tuple-element.18), channel_id=1, replica_groups=mesh['y'=4,'z'=16,'c'=2,'x'=4] {'x'}, dimensions={0} | all-to-all | bytes 262144 | tf_op jit(solution)/shard_map/all_to_all | solution.py:194
  131.3 3.1 %shard_map.89 = f32[4,64]{1,0:T(4,128)} custom-call(f32[4,64,128]{2,1,0:T(8,128)S(1)} %all_to_all.53.in_ref, f32[64,128]{1,0:T(8,128)S(1)} %get-tuple-element.16.side_ref), custom_call_target="tpu_custom_call" | custom-call | tf_op jit(solution)/shard_map/pallas_call | solution.py:255
  (9 shorter events, 0.2 us)
Async XLA Ops:
  0.6 1.4 %copy-start = (bf16[3072,256]{1,0:T(8,128)(2,1)S(1)}, bf16[3072,256]{1,0:T(8,128)(2,1)}, u32[]{:S(2)}) copy-start(bf16[3072,256]{1,0:T(8,128)(2,1)} %s_ref.3) | copy-start | bytes 4718596
  2.0 0.8 copy-start.2
  4.0 19.8 %copy-start.1 = (bf16[3072,256]{1,0:T(8,128)(2,1)S(1)}, bf16[3072,256]{1,0:T(8,128)(2,1)}, u32[]{:S(2)}) copy-start(bf16[3072,256]{1,0:T(8,128)(2,1)} %s_ref.3) | copy-start | bytes 4718596
  4.0 19.8 %copy-start.3 = (f32[64,256]{1,0:T(8,128)S(1)}, f32[64,256]{1,0:T(8,128)}, u32[]{:S(2)}) copy-start(f32[64,256]{1,0:T(8,128)} %v_ref.3) | copy-start | bytes 196612
  4.0 19.8 %copy-start.4 = (f32[64,64]{1,0:T(8,128)S(1)}, f32[64,64]{1,0:T(8,128)}, u32[]{:S(2)}) copy-start(f32[64,64]{1,0:T(8,128)} %h_ref.1) | copy-start | bytes 49156
  4.0 19.8 %copy-start.5 = (f32[64,4]{0,1:T(4,128)S(1)}, f32[64,4]{0,1:T(4,128)}, u32[]{:S(2)}) copy-start(f32[64,4]{0,1:T(4,128)} %param.11) | copy-start | bytes 3076
  4.0 19.8 %copy-start.6 = (s32[24]{0:T(128)S(1)}, s32[24]{0:T(128)}, u32[]{:S(2)}) copy-start(s32[24]{0:T(128)} %owner_ref.1) | copy-start | bytes 292
  4.0 19.8 %copy-start.7 = (s32[4]{0:T(128)S(1)}, s32[4]{0:T(128)}, u32[]{:S(2)}) copy-start(s32[4]{0:T(128)} %length_ref.1) | copy-start | bytes 52

commit v3 on v2

--- a/solution.py
+++ b/solution.py
@@ -22,6 +22,19 @@
 
 def mm_t(left, right):
     return lax.dot_general(left, right, LANES, precision=highest, preferred_element_type=jnp.float32)
+
+
+def halves(value):
+    high = value.astype(jnp.bfloat16)
+    return high, (value - high.astype(jnp.float32)).astype(jnp.bfloat16)
+
+
+def mm_halves(left, right, dims=(((1,), (0,)), ((), ()))):
+    rows, cols = left.shape[0], right.shape[1 - dims[0][1][0]]
+    left = jnp.concatenate(halves(left), axis=0)
+    right = jnp.concatenate(halves(right), axis=1 - dims[0][1][0])
+    terms = lax.dot_general(left, right, dims, preferred_element_type=jnp.float32)
+    return terms[0:rows, 0:cols] + (terms[0:rows, cols:] + terms[rows:, 0:cols])
 
 
 def eye_mask():
@@ -56,10 +69,24 @@
     return both
 
 
-def partial_kernel(v_ref, s_ref, out_ref):
-    out_ref[0] = lax.dot_general(
-        v_ref[...].astype(jnp.bfloat16), s_ref[...], LANES, preferred_element_type=jnp.float32
-    ).astype(jnp.bfloat16)
+def partial_kernel(v_ref, s_ref, out_ref, v_buf, s_buf, sems):
+    count, _, quarter = out_ref.shape
+    pieces = 2
+    step = count * quarter // pieces
+    copies = [pltpu.make_async_copy(v_ref, v_buf, sems.at[pieces])]
+    for i in range(pieces):
+        rows = pl.ds(i * step, step)
+        copies.append(pltpu.make_async_copy(s_ref.at[rows, :], s_buf.at[rows, :], sems.at[i]))
+    for copy in copies:
+        copy.start()
+    copies[0].wait()
+    factor_bf = v_buf[...].astype(jnp.bfloat16)
+    for i in range(pieces):
+        copies[i + 1].wait()
+        for peer in range(i * count // pieces, max((i + 1) * count // pieces, i * count // pieces + 1)):
+            out_ref[peer] = lax.dot_general(
+                factor_bf, s_buf[peer * quarter : (peer + 1) * quarter, :], LANES, preferred_element_type=jnp.float32
+            ).astype(jnp.bfloat16)
 
 
 def three(value):
@@ -70,64 +97,60 @@
 
 
 def polar_kernel(
-    owner_ref, length_ref, part_ref, s_ref, h_ref, v_ref, w_ref, proj_ref, pack_ref, p_ref, g_ref, t_ref, q_ref, *, peers, spread
+    owner_ref, length_ref, part_ref, s_ref, h_ref, v_ref, w_ref, proj_ref, pack_ref, p_ref, *, peers, spread
 ):
-    slots = s_ref.shape[0] // TILE
+    rows, width = s_ref.shape
+    slots = rows // TILE
     eye = eye_mask()
-    lane = lax.broadcasted_iota(jnp.int32, (R, TILE), 1)
-    starts = [jnp.int32(0)]
-    for k in range(1, KD):
-        total = jnp.int32(0)
-        for t in range(slots):
-            total = total + jnp.where(owner_ref[t] < k, 1, 0)
-        starts.append(total)
-    g_ref[...] = jnp.zeros_like(g_ref)
-    q_ref[...] = jnp.zeros_like(q_ref)
-    for t in range(slots):
-        own = owner_ref[t]
-        left = jnp.int32(0)
-        for k in range(KD):
-            left = jnp.where(own == k, length_ref[k] - (t - starts[k]) * TILE, left)
-        cols = slice(t * TILE, (t + 1) * TILE)
-        quarter, first = divmod(t * TILE, part_ref.shape[2])
-        value = part_ref[quarter, :, first : first + TILE]
-        value = jnp.where(lane < left, value.astype(jnp.float32), 0.0).astype(jnp.bfloat16)
-        p_ref[:, cols] = value
-        g_ref[own] += lax.dot_general(value, value, LANES, preferred_element_type=jnp.float32)
+    lane = lax.broadcasted_iota(jnp.int32, (1, rows), 1)
+    masks = []
+    for k in range(KD):
+        first = jnp.int32(0)
+        for t in range(slots if k > 0 else 0):
+            first = first + jnp.where(owner_ref[t] < k, TILE, 0)
+        live = (lane >= first) & (lane < first + length_ref[k])
+        masks.append(jnp.where(live, 1.0, 0.0).astype(jnp.bfloat16))
+    summed = jnp.concatenate([part_ref[peer] for peer in range(peers)], axis=1)
+    for k in range(KD):
+        p_ref[k * R : (k + 1) * R, :] = summed * masks[k]
+    products = lax.dot_general(summed, p_ref[...], LANES, preferred_element_type=jnp.float32)
     hmat = h_ref[...]
     wmat = w_ref[...].T
-    grams, turns = [], []
+    wide_eye = jnp.where(
+        lax.broadcasted_iota(jnp.int32, (R, 2 * R), 0) == lax.broadcasted_iota(jnp.int32, (R, 2 * R), 1), 1.5, 0.0
+    )
+    both = []
     for k in range(KD):
         mix = hmat * jnp.sum(jnp.where(eye, wmat[:, k : k + 1], 0.0), axis=0, keepdims=True)
-        gram = mm_t(mm(mix, g_ref[k]), mix)
+        gram = mm_t(mm(mix, products[:, k * R : (k + 1) * R]), mix)
         energy = jnp.sum(jnp.where(eye, gram, 0.0), keepdims=True)
         scale = lax.rsqrt(energy + 1e-06)
-        grams.append(gram * (scale * scale))
-        turns.append(mix * scale)
+        both.append(jnp.concatenate([gram * (scale * scale), mix * scale], axis=1))
     for iteration in range(ITERS):
-        steps = [jnp.where(eye, 1.5, 0.0) - 0.5 * gram for gram in grams]
-        turns = [mm(step, turn) for step, turn in zip(steps, turns)]
+        steps = [wide_eye - 0.5 * pair for pair in both]
+        both = [mm_halves(step[:, 0:R], pair) for step, pair in zip(steps, both)]
         if iteration < ITERS - 1:
-            halves = [mm(step, gram) for step, gram in zip(steps, grams)]
-            grams = [mm(half, step) for half, step in zip(halves, steps)]
-    t_ref[KD] = jnp.zeros_like(t_ref[KD])
-    for k in range(KD):
-        for i, term in enumerate(three(turns[k])):
-            t_ref[k, i] = term
-    for t in range(slots):
-        own = owner_ref[t]
-        cols = slice(t * TILE, (t + 1) * TILE)
-        value = p_ref[:, cols]
-        terms = [jnp.dot(t_ref[own, i], value, preferred_element_type=jnp.float32) for i in range(3)]
-        polar = (terms[0] + (terms[1] + terms[2])).astype(jnp.bfloat16)
-        q_ref[own] += jnp.dot(polar, s_ref[cols, :], preferred_element_type=jnp.float32)
+            next_grams = [mm_halves(pair[:, 0:R], step) for step, pair in zip(steps, both)]
+            first_half = lax.broadcasted_iota(jnp.int32, (R, 2 * R), 1) < R
+            both = [jnp.where(first_half, gram, pair) for gram, pair in zip(next_grams, both)]
+    parts = [three(pair[:, R : 2 * R]) for pair in both]
+    turn_rows = jnp.concatenate(
+        [jnp.concatenate([parts[k][i] for k in range(KD)], axis=1) for i in range(3)], axis=0
+    )
+    chunk = 2 * TILE
+    for first in range(0, rows, chunk):
+        cols = slice(first, first + chunk)
+        terms = jnp.dot(turn_rows, p_ref[:, cols], preferred_element_type=jnp.float32)
+        polar = (terms[0:R] + (terms[R : 2 * R] + terms[2 * R : 3 * R])).astype(jnp.bfloat16)
+        for k in range(KD):
+            p_ref[k * R : (k + 1) * R, cols] = polar * masks[k][:, cols]
+    projected = jnp.dot(p_ref[...], s_ref[...], preferred_element_type=jnp.float32)
     vmat = v_ref[...]
-    width = vmat.shape[1]
     head = jnp.zeros((R, R), jnp.float32)
     for k in range(KD):
-        block = q_ref[k]
+        block = projected[k * R : (k + 1) * R, :]
         proj_ref[:, k * width : (k + 1) * width] = block
-        head = head + mm_t(block, vmat * wmat[:, k : k + 1])
+        head = head + mm_halves(block, vmat * wmat[:, k : k + 1], LANES)
     pack_ref[0:R, :] = jnp.concatenate([head, mm_t(wmat, wmat) * (1.0 / peers)], axis=1)
     pack_ref[R : 2 * R, :] = jnp.concatenate(
         [mm_t(vmat, vmat) * (1.0 / spread), jnp.zeros((R, R), jnp.float32)], axis=1
@@ -137,11 +160,10 @@
 def head_kernel(pack_ref, proj_ref, w_ref, newh_ref, hp_ref, col_ref, side_ref):
     head, wgram = pack_ref[0:R, 0:R], pack_ref[0:R, R : 2 * R]
     fgram = pack_ref[R : 2 * R, 0:R]
-    eye = eye_mask()
     newh_t = eliminate(jnp.concatenate([fgram * wgram, head.T], axis=1))[:, R:]
     newh_ref[...] = newh_t.T
     wmat = w_ref[...].T
-    hp = mm(newh_t, proj_ref[...])
+    hp = mm_halves(newh_t, proj_ref[...])
     hp_ref[...] = hp
     width = hp.shape[1] // KD
     col = hp[:, 0:width] * wmat[:, 0:1]
@@ -150,14 +172,14 @@
     for half in range(width // TILE):
         col_ref[half * R : (half + 1) * R, :] = col[:, half * TILE : (half + 1) * TILE]
     hgram = mm_t(newh_t, newh_t)
-    inverse = eliminate(jnp.concatenate([hgram * wgram, jnp.where(eye, 1.0, 0.0)], axis=1))[:, R:]
+    inverse = eliminate(jnp.concatenate([hgram * wgram, jnp.where(eye_mask(), 1.0, 0.0)], axis=1))[:, R:]
     side_ref[...] = jnp.concatenate([hgram, inverse], axis=1)
 
 
-def column_kernel(col_ref, hp_ref, side_ref, newv_ref, out_ref):
+def column_kernel(col_ref, hp_ref, inverse_ref, newv_ref, out_ref):
     halves = col_ref.shape[0] // R
     col = jnp.concatenate([col_ref[half * R : (half + 1) * R, :] for half in range(halves)], axis=1)
-    newv = mm(side_ref[:, R : 2 * R], col)
+    newv = mm(inverse_ref[:, R : 2 * R], col)
     newv_ref[...] = newv
     width = newv.shape[1]
     lane = lax.broadcasted_iota(jnp.int32, (R, R), 1)
@@ -182,8 +204,8 @@
     return [pl.BlockSpec(memory_space=pltpu.VMEM)] * count
 
 
-def params():
-    return pltpu.CompilerParams(vmem_limit_bytes=48 * 1024 * 1024)
+def params(mib=48):
+    return pltpu.CompilerParams(vmem_limit_bytes=mib * 1024 * 1024)
 
 
 def f32(*shape):
@@ -206,14 +228,15 @@
     w_rows = weights_s.T
     parts = pl.pallas_call(
         partial_kernel,
-        grid=(nx,),
-        in_specs=[
-            pl.BlockSpec((R, width), lambda i: (0, 0)),
-            pl.BlockSpec((quarter, width), lambda i: (i, 0)),
+        in_specs=[pl.BlockSpec(memory_space=pltpu.HBM)] * 2,
+        out_specs=pl.BlockSpec(memory_space=pltpu.VMEM),
+        out_shape=jax.ShapeDtypeStruct((nx, R, quarter), jnp.bfloat16),
+        scratch_shapes=[
+            pltpu.VMEM((R, width), jnp.float32),
+            pltpu.VMEM((rows, width), jnp.bfloat16),
+            pltpu.SemaphoreType.DMA((nx + 1,)),
         ],
-        out_specs=pl.BlockSpec((1, R, quarter), lambda i: (i, 0, 0)),
-        out_shape=jax.ShapeDtypeStruct((nx, R, quarter), jnp.bfloat16),
-        compiler_params=params(),
+        compiler_params=params(63),
     )(factor_v, series)
     parts = jnp.sum(exchange(parts, "x").astype(jnp.float32), axis=0).astype(jnp.bfloat16)
     parts = share(parts, "x", nx)
@@ -223,10 +246,7 @@
         out_specs=vmem(2),
         out_shape=[f32(R, KD * width), f32(2 * R, 2 * R)],
         scratch_shapes=[
-            pltpu.VMEM((R, rows), jnp.bfloat16),
-            pltpu.VMEM((KD + 1, R, R), jnp.float32),
-            pltpu.VMEM((KD + 1, 3, R, R), jnp.bfloat16),
-            pltpu.VMEM((KD + 1, R, width), jnp.float32),
+            pltpu.VMEM((KD * R, rows), jnp.bfloat16),
         ],
         compiler_params=params(),
     )(tile_owner, lengths, parts, series, factor_h, factor_v, w_rows)

time: 135 us -> 133 us (0.985)
  local copies, waits for them, and re-layouts: 2.35 us -> 0.1 us
    unnamed x16 -> x12, local copies, waits for them, and re-layouts: 2.28 us -> 0.04 us
    pallas_call x1, Pallas kernels: 1.07 us -> 2.68 us  [body(): pl.pallas_call(partial_kernel, in_specs=[pl.BlockSpec(memory_space=pltpu....]
    pallas_call x1, Pallas kernels: 8.04 us -> 6.57 us  [body(): pl.pallas_call(functools.partial(polar_kernel, peers=nx, spread=ny * nz *...]
where the time goes in v3:
time: 133 us; the launch traced here: 132 us
  blocking collectives  113 us (85%)
  Pallas kernels  18.5 us (14%)
    all_to_all x9, blocking collectives, exchange(): return lax.all_to_all(value, axes, 0, 0, tiled=True)  113 us
    pallas_call x1, Pallas kernels, body(): pl.pallas_call(functools.partial(polar_kernel, peers=nx, spread=ny * nz *...  6.57 us
    pallas_call x1, Pallas kernels, body(): pl.pallas_call(head_kernel, in_specs=vmem(3), out_specs=vmem(4), out_shap...  5.26 us
    pallas_call x1, Pallas kernels, body(): pl.pallas_call(weight_kernel, in_specs=vmem(2), out_specs=pl.BlockSpec(me...  3.07 us
    pallas_call x1, Pallas kernels, body(): pl.pallas_call(partial_kernel, in_specs=[pl.BlockSpec(memory_space=pltpu....  2.68 us

profile of v3, /device:TPU:1, one launch (start us, length us, event | category | flops | bytes accessed | tf_op | source)
XLA Modules:
  0.0 132.5 jit_solution(6182577545790743363)
XLA Ops:
  0.6 2.7 %shard_map.85 = bf16[4,64,768]{2,1,0:T(8,128)(2,1)} custom-call(f32[64,256]{1,0:T(8,128)} %v_ref.3, bf16[3072,256]{1,0:T(8,128)(2,1)} %s_ref.3), custom_call_target="tpu_custom_call" | custom-call | tf_op jit(solution)/shard_map/pallas_call | solution.py:229
  3.3 0.0 copy-start
  3.3 0.0 copy-start.1
  3.3 0.0 copy-start.2
  3.4 0.0 copy-start.3
  3.4 0.0 copy-start.4
  3.4 0.0 copy-start.5
  3.4 11.2 %all_to_all.45 = bf16[4,64,768]{2,1,0:T(8,128)(2,1)S(1)} all-to-all(bf16[4,64,768]{2,1,0:T(8,128)(2,1)} %shard_map.85), channel_id=1, replica_groups=mesh['y'=4,'z'=16,'c'=2,'x'=4] {'x'}, dimensions={0} | all-to-all | bytes 786432 | tf_op jit(solution)/shard_map/all_to_all | solution.py:216
  14.6 0.1 reduce_sum.48
  14.7 8.6 %all_to_all.46.part_ref = bf16[4,64,768]{2,1,0:T(8,128)(2,1)S(1)} all-to-all(bf16[4,64,768]{2,1,0:T(8,128)(2,1)S(1)} %broadcast_in_dim.10), channel_id=1, replica_groups=mesh['y'=4,'z'=16,'c'=2,'x'=4] {'x'}, dimensions={0} | all-to-all | bytes 786432 | tf_op jit(solution)/shard_map/all_to_all | solution.py:216
  23.3 0.0 copy-done
  23.3 0.0 copy-done.1
  23.3 0.0 copy-done.2
  23.3 0.0 copy-done.3
  23.4 0.0 copy-done.4
  23.4 0.0 copy-done.5
  23.4 6.6 %shard_map.86 = (f32[64,1024]{1,0:T(8,128)S(1)}, f32[128,128]{1,0:T(8,128)S(1)}) custom-call(s32[24]{0:T(128)S(1)} %copy-done.4, s32[4]{0:T(128)S(1)} %copy-done.5, bf16[4,64,768]{2,1,0:T(8,128)(2,1)S(1)} %all_to_all.46.part_ref, bf16[3072,256]{1,0:T(8,128)(2,1)S(1)} %copy-done, f32[64,64]{1,0:T(8,128)S(1)} %copy-done.2, f32[64,256]{1,0:T(8,128)S(1)} %copy-done.1, ...), custom_call_target="tpu_custom_call" | custom-call | tf_op jit(solution)/shard_map/pallas_call | solution.py:243
  29.9 17.8 %all_to_all.47 = f32[32,4,128]{2,1,0:T(4,128)S(1)} all-to-all(f32[32,4,128]{2,1,0:T(4,128)S(1)} %bitcast.9), channel_id=1, replica_groups=mesh['y'=4,'z'=16,'c'=2,'x'=4] {'y','c','x'}, dimensions={0} | all-to-all | bytes 131072 | tf_op jit(solution)/shard_map/all_to_all | solution.py:216
  47.8 24.7 %all_to_all.48 = f32[16,4,128]{2,1,0:T(4,128)S(1)} all-to-all(f32[16,4,128]{2,1,0:T(4,128)S(1)} %broadcast_in_dim.11), channel_id=1, replica_groups=mesh['y'=4,'z'=16,'c'=2,'x'=4] {'z'}, dimensions={0} | all-to-all | bytes 65536 | tf_op jit(solution)/shard_map/all_to_all | solution.py:216
  72.5 12.4 %all_to_all.49 = f32[32,4,128]{2,1,0:T(4,128)S(1)} all-to-all(f32[32,4,128]{2,1,0:T(4,128)S(1)} %broadcast_in_dim.12), channel_id=1, replica_groups=mesh['y'=4,'z'=16,'c'=2,'x'=4] {'y','c','x'}, dimensions={0} | all-to-all | bytes 131072 | tf_op jit(solution)/shard_map/all_to_all | solution.py:216
  84.8 5.3 %shard_map.87 = (f32[64,64]{1,0:T(8,128)}, f32[64,1024]{1,0:T(8,128)S(1)}, f32[128,128]{1,0:T(8,128)S(1)}, f32[64,128]{1,0:T(8,128)S(1)}) custom-call(f32[128,128]{1,0:T(8,128)S(1)} %bitcast.6, f32[64,1024]{1,0:T(8,128)S(1)} %get-tuple-element.12.proj_ref, f32[4,64]{1,0:T(4,128)S(1)} %bitcast.11), custom_call_target="tpu_custom_call" | custom-call | tf_op jit(solution)/shard_map/pallas_call | solution.py:257
  90.1 7.6 %all_to_all.50 = f32[8,16,128]{2,1,0:T(8,128)S(1)} all-to-all(f32[8,16,128]{2,1,0:T(8,128)S(1)} %bitcast.8), channel_id=1, replica_groups=mesh['y'=4,'z'=16,'c'=2,'x'=4] {'y','c'}, dimensions={0} | all-to-all | bytes 131072 | tf_op jit(solution)/shard_map/all_to_all | solution.py:216
  97.8 14.2 %all_to_all.51 = bf16[16,16,128]{2,1,0:T(8,128)(2,1)S(1)} all-to-all(bf16[16,16,128]{2,1,0:T(8,128)(2,1)S(1)} %broadcast_in_dim.13), channel_id=1, replica_groups=mesh['y'=4,'z'=16,'c'=2,'x'=4] {'z'}, dimensions={0} | all-to-all | bytes 131072 | tf_op jit(solution)/shard_map/all_to_all | solution.py:216
  112.0 9.3 %all_to_all.52 = f32[8,16,128]{2,1,0:T(8,128)S(1)} all-to-all(f32[8,16,128]{2,1,0:T(8,128)S(1)} %broadcast_in_dim.14), channel_id=1, replica_groups=mesh['y'=4,'z'=16,'c'=2,'x'=4] {'y','c'}, dimensions={0} | all-to-all | bytes 131072 | tf_op jit(solution)/shard_map/all_to_all | solution.py:216
  121.3 0.9 shard_map.88
  122.2 7.2 %all_to_all.53.in_ref = f32[4,64,128]{2,1,0:T(8,128)S(1)} all-to-all(f32[4,64,128]{2,1,0:T(8,128)S(1)} %get-tuple-element.18), channel_id=1, replica_groups=mesh['y'=4,'z'=16,'c'=2,'x'=4] {'x'}, dimensions={0} | all-to-all | bytes 262144 | tf_op jit(solution)/shard_map/all_to_all | solution.py:216
  129.4 3.1 %shard_map.89 = f32[4,64]{1,0:T(4,128)} custom-call(f32[4,64,128]{2,1,0:T(8,128)S(1)} %all_to_all.53.in_ref, f32[64,128]{1,0:T(8,128)S(1)} %get-tuple-element.16.inverse_ref.side_ref), custom_call_target="tpu_custom_call" | custom-call | tf_op jit(solution)/shard_map/pallas_call | solution.py:275
  (9 shorter events, 0.2 us)
Async XLA Ops:
  3.3 20.0 %copy-start = (bf16[3072,256]{1,0:T(8,128)(2,1)S(1)}, bf16[3072,256]{1,0:T(8,128)(2,1)}, u32[]{:S(2)}) copy-start(bf16[3072,256]{1,0:T(8,128)(2,1)} %s_ref.3) | copy-start | bytes 4718596
  3.3 20.0 %copy-start.1 = (f32[64,256]{1,0:T(8,128)S(1)}, f32[64,256]{1,0:T(8,128)}, u32[]{:S(2)}) copy-start(f32[64,256]{1,0:T(8,128)} %v_ref.3) | copy-start | bytes 196612
  3.3 20.0 %copy-start.2 = (f32[64,64]{1,0:T(8,128)S(1)}, f32[64,64]{1,0:T(8,128)}, u32[]{:S(2)}) copy-start(f32[64,64]{1,0:T(8,128)} %h_ref.1) | copy-start | bytes 49156
  3.4 20.0 %copy-start.3 = (f32[64,4]{0,1:T(4,128)S(1)}, f32[64,4]{0,1:T(4,128)}, u32[]{:S(2)}) copy-start(f32[64,4]{0,1:T(4,128)} %param.11) | copy-start | bytes 3076
  3.4 20.0 %copy-start.4 = (s32[24]{0:T(128)S(1)}, s32[24]{0:T(128)}, u32[]{:S(2)}) copy-start(s32[24]{0:T(128)} %owner_ref.1) | copy-start | bytes 292
  3.4 20.0 %copy-start.5 = (s32[4]{0:T(128)S(1)}, s32[4]{0:T(128)}, u32[]{:S(2)}) copy-start(s32[4]{0:T(128)} %length_ref.1) | copy-start | bytes 52

commit v4 on v3

--- a/solution.py
+++ b/solution.py
@@ -43,28 +43,36 @@
     return rows == cols
 
 
-def eliminate(both):
+def eliminate(both, block=8):
     rows = lax.broadcasted_iota(jnp.int32, both.shape, 0)
-    for k in range(0, R, 4):
-        col = [jnp.broadcast_to(both[:, k + i : k + i + 1], both.shape) for i in range(4)]
-        row = [both[k + i : k + i + 1, :] for i in range(4)]
-        piv = [[col[j][k + i : k + i + 1, :] for j in range(4)] for i in range(4)]
-        inv = 1.0 / (piv[0][0] * piv[1][1] - piv[0][1] * piv[0][1])
-        a00, a01, a11 = piv[1][1] * inv, -piv[0][1] * inv, piv[0][0] * inv
-        e02, e12 = a00 * piv[0][2] + a01 * piv[1][2], a01 * piv[0][2] + a11 * piv[1][2]
-        e03, e13 = a00 * piv[0][3] + a01 * piv[1][3], a01 * piv[0][3] + a11 * piv[1][3]
-        s22 = piv[2][2] - (piv[0][2] * e02 + piv[1][2] * e12)
-        s23 = piv[2][3] - (piv[0][2] * e03 + piv[1][2] * e13)
-        s33 = piv[3][3] - (piv[0][3] * e03 + piv[1][3] * e13)
-        inv = 1.0 / (s22 * s33 - s23 * s23)
-        t2 = row[2] - e02 * row[0] - e12 * row[1]
-        t3 = row[3] - e03 * row[0] - e13 * row[1]
-        n2, n3 = (s33 * t2 - s23 * t3) * inv, (s22 * t3 - s23 * t2) * inv
-        n0 = (a00 * row[0] + a01 * row[1]) - e02 * n2 - e03 * n3
-        n1 = (a01 * row[0] + a11 * row[1]) - e12 * n2 - e13 * n3
-        rest = (both - col[0] * n0 - col[1] * n1) - (col[2] * n2 + col[3] * n3)
-        for i, new in enumerate((n0, n1, n2, n3)):
-            rest = jnp.where(rows == k + i, new, rest)
+    for k in range(0, R, block):
+        col = [jnp.broadcast_to(both[:, k + i : k + i + 1], both.shape) for i in range(block)]
+        row = [both[k + i : k + i + 1, :] for i in range(block)]
+        piv = [[col[j][k + i : k + i + 1, :] for j in range(block)] for i in range(block)]
+        for q in range(0, block, 2):
+            inv = 1.0 / (piv[q][q] * piv[q + 1][q + 1] - piv[q][q + 1] * piv[q + 1][q])
+            a00, a01 = piv[q + 1][q + 1] * inv, -piv[q][q + 1] * inv
+            a10, a11 = -piv[q + 1][q] * inv, piv[q][q] * inv
+            new0, new1 = a00 * row[q] + a01 * row[q + 1], a10 * row[q] + a11 * row[q + 1]
+            later = range(q + 2, block)
+            solved = {
+                j: (a00 * piv[q][j] + a01 * piv[q + 1][j], a10 * piv[q][j] + a11 * piv[q + 1][j])
+                for j in later
+            }
+            for i in range(block):
+                if i in (q, q + 1):
+                    continue
+                row[i] = row[i] - (piv[i][q] * new0 + piv[i][q + 1] * new1)
+                for j in later:
+                    piv[i][j] = piv[i][j] - (piv[i][q] * solved[j][0] + piv[i][q + 1] * solved[j][1])
+            row[q], row[q + 1] = new0, new1
+            for j in later:
+                piv[q][j], piv[q + 1][j] = solved[j]
+        rest = both
+        for i in range(0, block, 2):
+            rest = rest - (col[i] * row[i] + col[i + 1] * row[i + 1])
+        for i in range(block):
+            rest = jnp.where(rows == k + i, row[i], rest)
         both = rest
     return both
 
@@ -113,17 +121,25 @@
     summed = jnp.concatenate([part_ref[peer] for peer in range(peers)], axis=1)
     for k in range(KD):
         p_ref[k * R : (k + 1) * R, :] = summed * masks[k]
-    products = lax.dot_general(summed, p_ref[...], LANES, preferred_element_type=jnp.float32)
     hmat = h_ref[...]
     wmat = w_ref[...].T
+    hgram = lax.dot_general(
+        hmat, hmat, (((0,), (0,)), ((), ())), precision=highest, preferred_element_type=jnp.float32
+    )
+    products = lax.dot_general(summed, p_ref[...], LANES, preferred_element_type=jnp.float32)
     wide_eye = jnp.where(
         lax.broadcasted_iota(jnp.int32, (R, 2 * R), 0) == lax.broadcasted_iota(jnp.int32, (R, 2 * R), 1), 1.5, 0.0
     )
+    column_rows = [
+        jnp.sum(jnp.where(eye, wmat[:, k : k + 1], 0.0), axis=0, keepdims=True) for k in range(KD)
+    ]
     both = []
     for k in range(KD):
-        mix = hmat * jnp.sum(jnp.where(eye, wmat[:, k : k + 1], 0.0), axis=0, keepdims=True)
-        gram = mm_t(mm(mix, products[:, k * R : (k + 1) * R]), mix)
-        energy = jnp.sum(jnp.where(eye, gram, 0.0), keepdims=True)
+        column = wmat[:, k : k + 1]
+        mix = hmat * column_rows[k]
+        product = products[:, k * R : (k + 1) * R]
+        gram = mm_t(mm(mix, product), mix)
+        energy = jnp.sum(product * (hgram * column * column_rows[k]), keepdims=True)
         scale = lax.rsqrt(energy + 1e-06)
         both.append(jnp.concatenate([gram * (scale * scale), mix * scale], axis=1))
     for iteration in range(ITERS):
@@ -170,7 +186,7 @@
     for k in range(1, KD):
         col = col + hp[:, k * width : (k + 1) * width] * wmat[:, k : k + 1]
     for half in range(width // TILE):
-        col_ref[half * R : (half + 1) * R, :] = col[:, half * TILE : (half + 1) * TILE]
+        col_ref[half * R : (half + 1) * R, :] = col[:, half * TILE : (half + 1) * TILE].astype(jnp.bfloat16)
     hgram = mm_t(newh_t, newh_t)
     inverse = eliminate(jnp.concatenate([hgram * wgram, jnp.where(eye_mask(), 1.0, 0.0)], axis=1))[:, R:]
     side_ref[...] = jnp.concatenate([hgram, inverse], axis=1)
@@ -258,12 +274,12 @@
         head_kernel,
         in_specs=vmem(3),
         out_specs=vmem(4),
-        out_shape=[f32(R, R), f32(R, KD * width), f32(R * width // TILE, TILE), f32(R, 2 * R)],
+        out_shape=[f32(R, R), f32(R, KD * width), jax.ShapeDtypeStruct((R * width // TILE, TILE), jnp.bfloat16), f32(R, 2 * R)],
         compiler_params=params(),
     )(pieces.reshape(2 * R, 2 * R), proj, w_rows)
     near = ny * nc
     pieces = exchange(col.reshape(near, col.shape[0] // near, TILE), ("y", "c"))
-    pieces = share(jnp.sum(pieces, axis=0).astype(jnp.bfloat16), "z", nz).astype(jnp.float32)
+    pieces = share(jnp.sum(pieces.astype(jnp.float32), axis=0).astype(jnp.bfloat16), "z", nz).astype(jnp.float32)
     pieces = share(jnp.sum(pieces, axis=0), ("y", "c"), near)
     new_v, sums = pl.pallas_call(
         column_kernel,

time: 133 us -> 131 us (0.985)
  Pallas kernels: 18.5 us -> 16.4 us
    pallas_call x1, Pallas kernels: 5.26 us -> 3.92 us  [body(): pl.pallas_call(head_kernel, in_specs=vmem(3), out_specs=vmem(4), out_shap...]
where the time goes in v4:
time: 131 us; the launch traced here: 130 us
  blocking collectives  113 us (86%)
  Pallas kernels  16.4 us (13%)
    all_to_all x9, blocking collectives, exchange(): return lax.all_to_all(value, axes, 0, 0, tiled=True)  113 us
    pallas_call x1, Pallas kernels, body(): pl.pallas_call(functools.partial(polar_kernel, peers=nx, spread=ny * nz *...  6.51 us
    pallas_call x1, Pallas kernels, body(): pl.pallas_call(head_kernel, in_specs=vmem(3), out_specs=vmem(4), out_shap...  3.92 us
    pallas_call x1, Pallas kernels, body(): pl.pallas_call(partial_kernel, in_specs=[pl.BlockSpec(memory_space=pltpu....  2.68 us

profile of v4, /device:TPU:1, one launch (start us, length us, event | category | flops | bytes accessed | tf_op | source)
XLA Modules:
  0.0 130.2 jit_solution(742738073618448105)
XLA Ops:
  0.6 2.7 %shard_map.85 = bf16[4,64,768]{2,1,0:T(8,128)(2,1)} custom-call(f32[64,256]{1,0:T(8,128)} %v_ref.3, bf16[3072,256]{1,0:T(8,128)(2,1)} %s_ref.3), custom_call_target="tpu_custom_call" | custom-call | tf_op jit(solution)/shard_map/pallas_call | solution.py:245
  3.3 0.0 copy-start
  3.3 0.0 copy-start.1
  3.3 0.0 copy-start.2
  3.4 0.0 copy-start.3
  3.4 0.0 copy-start.4
  3.4 0.0 copy-start.5
  3.4 11.2 %all_to_all.45 = bf16[4,64,768]{2,1,0:T(8,128)(2,1)S(1)} all-to-all(bf16[4,64,768]{2,1,0:T(8,128)(2,1)} %shard_map.85), channel_id=1, replica_groups=mesh['y'=4,'z'=16,'c'=2,'x'=4] {'x'}, dimensions={0} | all-to-all | bytes 786432 | tf_op jit(solution)/shard_map/all_to_all | solution.py:232
  14.6 0.1 reduce_sum.51
  14.7 8.6 %all_to_all.46.part_ref = bf16[4,64,768]{2,1,0:T(8,128)(2,1)S(1)} all-to-all(bf16[4,64,768]{2,1,0:T(8,128)(2,1)S(1)} %broadcast_in_dim.10), channel_id=1, replica_groups=mesh['y'=4,'z'=16,'c'=2,'x'=4] {'x'}, dimensions={0} | all-to-all | bytes 786432 | tf_op jit(solution)/shard_map/all_to_all | solution.py:232
  23.3 0.0 copy-done
  23.3 0.0 copy-done.1
  23.3 0.0 copy-done.2
  23.3 0.0 copy-done.3
  23.4 0.0 copy-done.4
  23.4 0.0 copy-done.5
  23.4 6.5 %shard_map.86 = (f32[64,1024]{1,0:T(8,128)S(1)}, f32[128,128]{1,0:T(8,128)S(1)}) custom-call(s32[24]{0:T(128)S(1)} %copy-done.4, s32[4]{0:T(128)S(1)} %copy-done.5, bf16[4,64,768]{2,1,0:T(8,128)(2,1)S(1)} %all_to_all.46.part_ref, bf16[3072,256]{1,0:T(8,128)(2,1)S(1)} %copy-done, f32[64,64]{1,0:T(8,128)S(1)} %copy-done.2, f32[64,256]{1,0:T(8,128)S(1)} %copy-done.1, ...), custom_call_target="tpu_custom_call" | custom-call | tf_op jit(solution)/shard_map/pallas_call | solution.py:259
  29.9 17.8 %all_to_all.47 = f32[32,4,128]{2,1,0:T(4,128)S(1)} all-to-all(f32[32,4,128]{2,1,0:T(4,128)S(1)} %bitcast.8), channel_id=1, replica_groups=mesh['y'=4,'z'=16,'c'=2,'x'=4] {'y','c','x'}, dimensions={0} | all-to-all | bytes 131072 | tf_op jit(solution)/shard_map/all_to_all | solution.py:232
  47.7 24.7 %all_to_all.48 = f32[16,4,128]{2,1,0:T(4,128)S(1)} all-to-all(f32[16,4,128]{2,1,0:T(4,128)S(1)} %broadcast_in_dim.11), channel_id=1, replica_groups=mesh['y'=4,'z'=16,'c'=2,'x'=4] {'z'}, dimensions={0} | all-to-all | bytes 65536 | tf_op jit(solution)/shard_map/all_to_all | solution.py:232
  72.4 12.4 %all_to_all.49 = f32[32,4,128]{2,1,0:T(4,128)S(1)} all-to-all(f32[32,4,128]{2,1,0:T(4,128)S(1)} %broadcast_in_dim.12), channel_id=1, replica_groups=mesh['y'=4,'z'=16,'c'=2,'x'=4] {'y','c','x'}, dimensions={0} | all-to-all | bytes 131072 | tf_op jit(solution)/shard_map/all_to_all | solution.py:232
  84.8 3.9 %shard_map.87 = (f32[64,64]{1,0:T(8,128)}, f32[64,1024]{1,0:T(8,128)S(1)}, bf16[128,128]{1,0:T(8,128)(2,1)S(1)}, f32[64,128]{1,0:T(8,128)S(1)}) custom-call(f32[128,128]{1,0:T(8,128)S(1)} %bitcast.6, f32[64,1024]{1,0:T(8,128)S(1)} %get-tuple-element.12.proj_ref, f32[4,64]{1,0:T(4,128)S(1)} %bitcast.11), custom_call_target="tpu_custom_call" | custom-call | tf_op jit(solution)/shard_map/pallas_call | solution.py:273
  88.7 7.5 %all_to_all.50 = bf16[8,16,128]{2,1,0:T(8,128)(2,1)S(1)} all-to-all(bf16[8,16,128]{2,1,0:T(8,128)(2,1)S(1)} %bitcast.9), channel_id=1, replica_groups=mesh['y'=4,'z'=16,'c'=2,'x'=4] {'y','c'}, dimensions={0} | all-to-all | bytes 65536 | tf_op jit(solution)/shard_map/all_to_all | solution.py:232
  96.2 14.2 %all_to_all.51 = bf16[16,16,128]{2,1,0:T(8,128)(2,1)S(1)} all-to-all(bf16[16,16,128]{2,1,0:T(8,128)(2,1)S(1)} %broadcast_in_dim.13), channel_id=1, replica_groups=mesh['y'=4,'z'=16,'c'=2,'x'=4] {'z'}, dimensions={0} | all-to-all | bytes 131072 | tf_op jit(solution)/shard_map/all_to_all | solution.py:232
  110.5 9.2 %all_to_all.52 = f32[8,16,128]{2,1,0:T(8,128)S(1)} all-to-all(f32[8,16,128]{2,1,0:T(8,128)S(1)} %broadcast_in_dim.14), channel_id=1, replica_groups=mesh['y'=4,'z'=16,'c'=2,'x'=4] {'y','c'}, dimensions={0} | all-to-all | bytes 131072 | tf_op jit(solution)/shard_map/all_to_all | solution.py:232
  119.7 0.9 shard_map.88
  120.6 7.2 %all_to_all.53.in_ref = f32[4,64,128]{2,1,0:T(8,128)S(1)} all-to-all(f32[4,64,128]{2,1,0:T(8,128)S(1)} %get-tuple-element.18), channel_id=1, replica_groups=mesh['y'=4,'z'=16,'c'=2,'x'=4] {'x'}, dimensions={0} | all-to-all | bytes 262144 | tf_op jit(solution)/shard_map/all_to_all | solution.py:232
  127.8 2.4 %shard_map.89 = f32[4,64]{1,0:T(4,128)} custom-call(f32[4,64,128]{2,1,0:T(8,128)S(1)} %all_to_all.53.in_ref, f32[64,128]{1,0:T(8,128)S(1)} %get-tuple-element.16.inverse_ref.side_ref), custom_call_target="tpu_custom_call" | custom-call | tf_op jit(solution)/shard_map/pallas_call | solution.py:291
  (9 shorter events, 0.2 us)
Async XLA Ops:
  3.3 20.0 %copy-start = (bf16[3072,256]{1,0:T(8,128)(2,1)S(1)}, bf16[3072,256]{1,0:T(8,128)(2,1)}, u32[]{:S(2)}) copy-start(bf16[3072,256]{1,0:T(8,128)(2,1)} %s_ref.3) | copy-start | bytes 4718596
  3.3 20.0 %copy-start.1 = (f32[64,256]{1,0:T(8,128)S(1)}, f32[64,256]{1,0:T(8,128)}, u32[]{:S(2)}) copy-start(f32[64,256]{1,0:T(8,128)} %v_ref.3) | copy-start | bytes 196612
  3.3 20.0 %copy-start.2 = (f32[64,64]{1,0:T(8,128)S(1)}, f32[64,64]{1,0:T(8,128)}, u32[]{:S(2)}) copy-start(f32[64,64]{1,0:T(8,128)} %h_ref.1) | copy-start | bytes 49156
  3.4 20.0 %copy-start.3 = (f32[64,4]{0,1:T(4,128)S(1)}, f32[64,4]{0,1:T(4,128)}, u32[]{:S(2)}) copy-start(f32[64,4]{0,1:T(4,128)} %param.11) | copy-start | bytes 3076
  3.4 20.0 %copy-start.4 = (s32[24]{0:T(128)S(1)}, s32[24]{0:T(128)}, u32[]{:S(2)}) copy-start(s32[24]{0:T(128)} %owner_ref.1) | copy-start | bytes 292
  3.4 20.0 %copy-start.5 = (s32[4]{0:T(128)S(1)}, s32[4]{0:T(128)}, u32[]{:S(2)}) copy-start(s32[4]{0:T(128)} %length_ref.1) | copy-start | bytes 52

commit v5 on v4

--- a/solution.py
+++ b/solution.py
@@ -105,7 +105,7 @@
 
 
 def polar_kernel(
-    owner_ref, length_ref, part_ref, s_ref, h_ref, v_ref, w_ref, proj_ref, pack_ref, p_ref, *, peers, spread
+    owner_ref, length_ref, part_ref, s_ref, h_ref, v_ref, w_ref, proj_ref, send_ref, p_ref, *, peers
 ):
     rows, width = s_ref.shape
     slots = rows // TILE
@@ -167,15 +167,76 @@
         block = projected[k * R : (k + 1) * R, :]
         proj_ref[:, k * width : (k + 1) * width] = block
         head = head + mm_halves(block, vmat * wmat[:, k : k + 1], LANES)
-    pack_ref[0:R, :] = jnp.concatenate([head, mm_t(wmat, wmat) * (1.0 / peers)], axis=1)
-    pack_ref[R : 2 * R, :] = jnp.concatenate(
-        [mm_t(vmat, vmat) * (1.0 / spread), jnp.zeros((R, R), jnp.float32)], axis=1
-    )
-
-
-def head_kernel(pack_ref, proj_ref, w_ref, newh_ref, hp_ref, col_ref, side_ref):
-    head, wgram = pack_ref[0:R, 0:R], pack_ref[0:R, R : 2 * R]
-    fgram = pack_ref[R : 2 * R, 0:R]
+    high, middle, low = [term.astype(jnp.float32) for term in three(w_ref[...])]
+    send_ref[...] = jnp.concatenate(
+        [
+            fold(head),
+            jnp.concatenate([high, middle], axis=1),
+            jnp.concatenate([low, jnp.zeros_like(low)], axis=1),
+        ],
+        axis=0,
+    ).astype(jnp.bfloat16)
+
+
+def fold(value):
+    return jnp.concatenate([value[0 : R // 2], value[R // 2 :]], axis=1)
+
+
+def unfold(value):
+    return jnp.concatenate([value[:, 0:R], value[:, R : 2 * R]], axis=0)
+
+
+def wide_halves(value):
+    return jnp.concatenate([half.astype(jnp.float32) for half in halves(value)], axis=1)
+
+
+def middle_kernel(in_ref, v_ref, out_ref, w_buf, gram_buf, *, sizes):
+    ny, nz, nc, nx = sizes
+    head = jnp.zeros((R // 2, 2 * R), jnp.float32)
+    for peer in range(nz):
+        value = in_ref[peer].astype(jnp.float32)
+        head = head + value[0 : R // 2]
+        first, last = value[R // 2 : R // 2 + KD], value[R // 2 + KD :]
+        w_buf[peer * KD : (peer + 1) * KD, :] = first[:, 0:R] + (first[:, R:] + last[:, 0:R])
+    weights = w_buf[...]
+    gram_buf[0:R, :] = lax.dot_general(
+        weights, weights, (((0,), (0,)), ((), ())), precision=highest, preferred_element_type=jnp.float32
+    )
+    vmat = v_ref[...]
+    gram_buf[R : 2 * R, :] = mm_t(vmat, vmat)
+    w_rows, v_rows = R // nx, R // (ny * nc)
+    place = lax.axis_index("y") * nc + lax.axis_index("c")
+    w_first = pl.multiple_of(lax.axis_index("x") * w_rows, w_rows)
+    v_first = pl.multiple_of(R + place * v_rows, v_rows)
+    parts = [
+        head,
+        wide_halves(gram_buf[pl.ds(w_first, w_rows), :]),
+        wide_halves(gram_buf[pl.ds(v_first, v_rows), :]),
+    ]
+    spare = out_ref.shape[1] - R // 2 - w_rows - v_rows
+    if spare:
+        parts.append(jnp.zeros((spare, 2 * R), jnp.float32))
+    value = jnp.concatenate(parts, axis=0).astype(jnp.bfloat16)
+    for peer in range(out_ref.shape[0]):
+        out_ref[peer] = value
+
+
+def head_kernel(pack_ref, proj_ref, w_ref, newh_ref, hp_ref, col_ref, side_ref, *, sizes):
+    ny, _, nc, nx = sizes
+    w_rows, v_rows = R // nx, R // (ny * nc)
+    head = jnp.zeros((R // 2, 2 * R), jnp.float32)
+    w_parts, v_parts = [0.0] * nx, [0.0] * (ny * nc)
+    for peer in range(pack_ref.shape[0]):
+        value = pack_ref[peer].astype(jnp.float32)
+        place, x = divmod(peer, nx)
+        w_last = R // 2 + w_rows
+        head = head + value[0 : R // 2]
+        w_parts[x] = w_parts[x] + value[R // 2 : w_last]
+        v_parts[place] = v_parts[place] + value[w_last : w_last + v_rows]
+    head = unfold(head)
+    wgram, fgram = [
+        jnp.concatenate([part[:, 0:R] + part[:, R:] for part in parts], axis=0) for parts in (w_parts, v_parts)
+    ]
     newh_t = eliminate(jnp.concatenate([fgram * wgram, head.T], axis=1))[:, R:]
     newh_ref[...] = newh_t.T
     wmat = w_ref[...].T
@@ -256,27 +317,34 @@
     )(factor_v, series)
     parts = jnp.sum(exchange(parts, "x").astype(jnp.float32), axis=0).astype(jnp.bfloat16)
     parts = share(parts, "x", nx)
-    proj, pack = pl.pallas_call(
-        functools.partial(polar_kernel, peers=nx, spread=ny * nz * nc),
+    proj, send = pl.pallas_call(
+        functools.partial(polar_kernel, peers=nx),
         in_specs=[pl.BlockSpec(memory_space=pltpu.SMEM)] * 2 + vmem(5),
         out_specs=vmem(2),
-        out_shape=[f32(R, KD * width), f32(2 * R, 2 * R)],
+        out_shape=[f32(R, KD * width), jax.ShapeDtypeStruct((R // 2 + 2 * KD, 2 * R), jnp.bfloat16)],
         scratch_shapes=[
             pltpu.VMEM((KD * R, rows), jnp.bfloat16),
         ],
         compiler_params=params(),
     )(tile_owner, lengths, parts, series, factor_h, factor_v, w_rows)
     near = ny * nc * nx
-    pieces = exchange(pack.reshape(near, 2 * R // near, 2 * R), ("y", "c", "x"))
-    pieces = share(jnp.sum(pieces, axis=0), "z", nz)
-    pieces = share(jnp.sum(pieces, axis=0), ("y", "c", "x"), near)
+    share_rows = -(-(R // 2 + R // nx + R // (ny * nc)) // 16) * 16
+    pieces = pl.pallas_call(
+        functools.partial(middle_kernel, sizes=sizes),
+        in_specs=vmem(2),
+        out_specs=pl.BlockSpec(memory_space=pltpu.VMEM),
+        out_shape=jax.ShapeDtypeStruct((near, share_rows, 2 * R), jnp.bfloat16),
+        scratch_shapes=[pltpu.VMEM((nz * KD, R), jnp.float32), pltpu.VMEM((2 * R, R), jnp.float32)],
+        compiler_params=params(),
+    )(share(send, "z", nz), factor_v)
+    pieces = exchange(pieces, ("y", "c", "x"))
     new_h, hp, col, side = pl.pallas_call(
-        head_kernel,
+        functools.partial(head_kernel, sizes=sizes),
         in_specs=vmem(3),
         out_specs=vmem(4),
         out_shape=[f32(R, R), f32(R, KD * width), jax.ShapeDtypeStruct((R * width // TILE, TILE), jnp.bfloat16), f32(R, 2 * R)],
         compiler_params=params(),
-    )(pieces.reshape(2 * R, 2 * R), proj, w_rows)
+    )(pieces, proj, w_rows)
     near = ny * nc
     pieces = exchange(col.reshape(near, col.shape[0] // near, TILE), ("y", "c"))
     pieces = share(jnp.sum(pieces.astype(jnp.float32), axis=0).astype(jnp.bfloat16), "z", nz).astype(jnp.float32)

time: 131 us -> 127 us (0.969)
  blocking collectives: 113 us -> 109 us
    all_to_all x9 -> x8, blocking collectives: 113 us -> 109 us  [exchange(): return lax.all_to_all(value, axes, 0, 0, tiled=True)]
    pallas_call x2 -> x3, Pallas kernels: 10.4 us -> 10.9 us  [the longest x1 6.35 us: body(): pl.pallas_call(functools.partial(polar_kernel, peers=nx), in_specs=[pl.Bl...]
where the time goes in v5:
time: 127 us; the launch traced here: 126 us
  blocking collectives  109 us (86%)
  Pallas kernels  16.9 us (13%)
    all_to_all x8, blocking collectives, exchange(): return lax.all_to_all(value, axes, 0, 0, tiled=True)  109 us
    pallas_call x1, Pallas kernels, body(): pl.pallas_call(functools.partial(polar_kernel, peers=nx), in_specs=[pl.Bl...  6.35 us
    pallas_call x1, Pallas kernels, body(): pl.pallas_call(functools.partial(head_kernel, sizes=sizes), in_specs=vmem...  4.02 us
    pallas_call x1, Pallas kernels, body(): pl.pallas_call(partial_kernel, in_specs=[pl.BlockSpec(memory_space=pltpu....  2.68 us

profile of v5, /device:TPU:1, one launch (start us, length us, event | category | flops | bytes accessed | tf_op | source)
XLA Modules:
  0.0 126.4 jit_solution(4947333214142386249)
XLA Ops:
  0.6 2.7 %shard_map.85 = bf16[4,64,768]{2,1,0:T(8,128)(2,1)} custom-call(f32[64,256]{1,0:T(8,128)} %v_ref.5, bf16[3072,256]{1,0:T(8,128)(2,1)} %s_ref.3), custom_call_target="tpu_custom_call" | custom-call | tf_op jit(solution)/shard_map/pallas_call | solution.py:306
  3.3 0.0 copy-start
  3.3 0.0 copy-start.1
  3.3 0.0 copy-start.2
  3.4 0.0 copy-start.3
  3.4 0.0 copy-start.4
  3.4 0.0 copy-start.5
  3.4 11.2 %all_to_all.40 = bf16[4,64,768]{2,1,0:T(8,128)(2,1)S(1)} all-to-all(bf16[4,64,768]{2,1,0:T(8,128)(2,1)} %shard_map.85), channel_id=1, replica_groups=mesh['y'=4,'z'=16,'c'=2,'x'=4] {'x'}, dimensions={0} | all-to-all | bytes 786432 | tf_op jit(solution)/shard_map/all_to_all | solution.py:293
  14.6 0.1 reduce_sum.33
  14.7 8.6 %all_to_all.41.part_ref = bf16[4,64,768]{2,1,0:T(8,128)(2,1)S(1)} all-to-all(bf16[4,64,768]{2,1,0:T(8,128)(2,1)S(1)} %broadcast_in_dim.8), channel_id=1, replica_groups=mesh['y'=4,'z'=16,'c'=2,'x'=4] {'x'}, dimensions={0} | all-to-all | bytes 786432 | tf_op jit(solution)/shard_map/all_to_all | solution.py:293
  23.3 0.0 copy-done
  23.3 0.0 copy-done.1
  23.3 0.0 copy-done.2
  23.3 0.0 copy-done.3
  23.4 0.0 copy-done.4
  23.4 0.0 copy-done.5
  23.4 6.4 %shard_map.86 = (f32[64,1024]{1,0:T(8,128)S(1)}, bf16[40,128]{1,0:T(8,128)(2,1)S(1)}) custom-call(s32[24]{0:T(128)S(1)} %copy-done.4, s32[4]{0:T(128)S(1)} %copy-done.5, bf16[4,64,768]{2,1,0:T(8,128)(2,1)S(1)} %all_to_all.41.part_ref, bf16[3072,256]{1,0:T(8,128)(2,1)S(1)} %copy-done, f32[64,64]{1,0:T(8,128)S(1)} %copy-done.2, f32[64,256]{1,0:T(8,128)S(1)} %copy-done.1, ...), custom_call_target="tpu_custom_call" | custom-call | tf_op jit(solution)/shard_map/pallas_call | solution.py:320
  29.8 27.8 %all_to_all.42.in_ref = bf16[16,40,128]{2,1,0:T(8,128)(2,1)S(1)} all-to-all(bf16[16,40,128]{2,1,0:T(8,128)(2,1)S(1)} %broadcast_in_dim.9), channel_id=1, replica_groups=mesh['y'=4,'z'=16,'c'=2,'x'=4] {'z'}, dimensions={0} | all-to-all | bytes 327680 | tf_op jit(solution)/shard_map/all_to_all | solution.py:293
  57.6 0.5 shard_map.87
  58.1 21.3 %all_to_all.43.pack_ref = bf16[32,64,128]{2,1,0:T(8,128)(2,1)S(1)} all-to-all(bf16[32,64,128]{2,1,0:T(8,128)(2,1)S(1)} %shard_map.87), channel_id=1, replica_groups=mesh['y'=4,'z'=16,'c'=2,'x'=4] {'y','c','x'}, dimensions={0} | all-to-all | bytes 1048576 | tf_op jit(solution)/shard_map/all_to_all | solution.py:293
  79.4 4.0 %shard_map.88 = (f32[64,64]{1,0:T(8,128)}, f32[64,1024]{1,0:T(8,128)S(1)}, bf16[128,128]{1,0:T(8,128)(2,1)S(1)}, f32[64,128]{1,0:T(8,128)S(1)}) custom-call(bf16[32,64,128]{2,1,0:T(8,128)(2,1)S(1)} %all_to_all.43.pack_ref, f32[64,1024]{1,0:T(8,128)S(1)} %get-tuple-element.12.proj_ref, f32[4,64]{1,0:T(4,128)S(1)} %bitcast.7), custom_call_target="tpu_custom_call" | custom-call | tf_op jit(solution)/shard_map/pallas_call | solution.py:341
  83.4 7.8 %all_to_all.44 = bf16[8,16,128]{2,1,0:T(8,128)(2,1)S(1)} all-to-all(bf16[8,16,128]{2,1,0:T(8,128)(2,1)S(1)} %bitcast.5), channel_id=1, replica_groups=mesh['y'=4,'z'=16,'c'=2,'x'=4] {'y','c'}, dimensions={0} | all-to-all | bytes 65536 | tf_op jit(solution)/shard_map/all_to_all | solution.py:293
  91.3 15.2 %all_to_all.45 = bf16[16,16,128]{2,1,0:T(8,128)(2,1)S(1)} all-to-all(bf16[16,16,128]{2,1,0:T(8,128)(2,1)S(1)} %broadcast_in_dim.10), channel_id=1, replica_groups=mesh['y'=4,'z'=16,'c'=2,'x'=4] {'z'}, dimensions={0} | all-to-all | bytes 131072 | tf_op jit(solution)/shard_map/all_to_all | solution.py:293
  106.5 9.4 %all_to_all.46 = f32[8,16,128]{2,1,0:T(8,128)S(1)} all-to-all(f32[8,16,128]{2,1,0:T(8,128)S(1)} %broadcast_in_dim.11), channel_id=1, replica_groups=mesh['y'=4,'z'=16,'c'=2,'x'=4] {'y','c'}, dimensions={0} | all-to-all | bytes 131072 | tf_op jit(solution)/shard_map/all_to_all | solution.py:293
  115.9 0.9 shard_map.89
  116.8 7.2 %all_to_all.47.in_ref = f32[4,64,128]{2,1,0:T(8,128)S(1)} all-to-all(f32[4,64,128]{2,1,0:T(8,128)S(1)} %get-tuple-element.18), channel_id=1, replica_groups=mesh['y'=4,'z'=16,'c'=2,'x'=4] {'x'}, dimensions={0} | all-to-all | bytes 262144 | tf_op jit(solution)/shard_map/all_to_all | solution.py:293
  124.0 2.4 %shard_map.90 = f32[4,64]{1,0:T(4,128)} custom-call(f32[4,64,128]{2,1,0:T(8,128)S(1)} %all_to_all.47.in_ref, f32[64,128]{1,0:T(8,128)S(1)} %get-tuple-element.16.inverse_ref.side_ref), custom_call_target="tpu_custom_call" | custom-call | tf_op jit(solution)/shard_map/pallas_call | solution.py:359
  (6 shorter events, 0.1 us)
Async XLA Ops:
  3.3 20.0 %copy-start = (bf16[3072,256]{1,0:T(8,128)(2,1)S(1)}, bf16[3072,256]{1,0:T(8,128)(2,1)}, u32[]{:S(2)}) copy-start(bf16[3072,256]{1,0:T(8,128)(2,1)} %s_ref.3) | copy-start | bytes 4718596
  3.3 20.0 %copy-start.1 = (f32[64,256]{1,0:T(8,128)S(1)}, f32[64,256]{1,0:T(8,128)}, u32[]{:S(2)}) copy-start(f32[64,256]{1,0:T(8,128)} %v_ref.5) | copy-start | bytes 196612
  3.3 20.0 %copy-start.2 = (f32[64,64]{1,0:T(8,128)S(1)}, f32[64,64]{1,0:T(8,128)}, u32[]{:S(2)}) copy-start(f32[64,64]{1,0:T(8,128)} %h_ref.1) | copy-start | bytes 49156
  3.4 20.0 %copy-start.3 = (f32[64,4]{0,1:T(4,128)S(1)}, f32[64,4]{0,1:T(4,128)}, u32[]{:S(2)}) copy-start(f32[64,4]{0,1:T(4,128)} %param.11) | copy-start | bytes 3076
  3.4 20.0 %copy-start.4 = (s32[24]{0:T(128)S(1)}, s32[24]{0:T(128)}, u32[]{:S(2)}) copy-start(s32[24]{0:T(128)} %owner_ref.1) | copy-start | bytes 292
  3.4 20.0 %copy-start.5 = (s32[4]{0:T(128)S(1)}, s32[4]{0:T(128)}, u32[]{:S(2)}) copy-start(s32[4]{0:T(128)} %length_ref.1) | copy-start | bytes 52

commit v6 on v5

--- a/solution.py
+++ b/solution.py
@@ -105,7 +105,7 @@
 
 
 def polar_kernel(
-    owner_ref, length_ref, part_ref, s_ref, h_ref, v_ref, w_ref, proj_ref, send_ref, p_ref, *, peers
+    owner_ref, length_ref, part_ref, s_ref, h_ref, w_ref, proj_ref, send_ref, p_ref, head_buf, *, peers
 ):
     rows, width = s_ref.shape
     slots = rows // TILE
@@ -161,16 +161,18 @@
         for k in range(KD):
             p_ref[k * R : (k + 1) * R, cols] = polar * masks[k][:, cols]
     projected = jnp.dot(p_ref[...], s_ref[...], preferred_element_type=jnp.float32)
-    vmat = v_ref[...]
+    heads = lax.dot_general(p_ref[...], summed, LANES, preferred_element_type=jnp.float32)
     head = jnp.zeros((R, R), jnp.float32)
     for k in range(KD):
-        block = projected[k * R : (k + 1) * R, :]
-        proj_ref[:, k * width : (k + 1) * width] = block
-        head = head + mm_halves(block, vmat * wmat[:, k : k + 1], LANES)
+        proj_ref[:, k * width : (k + 1) * width] = projected[k * R : (k + 1) * R, :]
+        head = head + heads[k * R : (k + 1) * R, :] * column_rows[k]
+    head_buf[...] = head
+    share_rows = R // peers
+    first = pl.multiple_of(lax.axis_index("x") * share_rows, share_rows)
     high, middle, low = [term.astype(jnp.float32) for term in three(w_ref[...])]
     send_ref[...] = jnp.concatenate(
         [
-            fold(head),
+            fold(head_buf[pl.ds(first, share_rows), :]),
             jnp.concatenate([high, middle], axis=1),
             jnp.concatenate([low, jnp.zeros_like(low)], axis=1),
         ],
@@ -179,7 +181,8 @@
 
 
 def fold(value):
-    return jnp.concatenate([value[0 : R // 2], value[R // 2 :]], axis=1)
+    half = value.shape[0] // 2
+    return jnp.concatenate([value[0:half], value[half:]], axis=1)
 
 
 def unfold(value):
@@ -192,11 +195,12 @@
 
 def middle_kernel(in_ref, v_ref, out_ref, w_buf, gram_buf, *, sizes):
     ny, nz, nc, nx = sizes
-    head = jnp.zeros((R // 2, 2 * R), jnp.float32)
+    h_rows = R // nx // 2
+    head = jnp.zeros((h_rows, 2 * R), jnp.float32)
     for peer in range(nz):
         value = in_ref[peer].astype(jnp.float32)
-        head = head + value[0 : R // 2]
-        first, last = value[R // 2 : R // 2 + KD], value[R // 2 + KD :]
+        head = head + value[0:h_rows]
+        first, last = value[h_rows : h_rows + KD], value[h_rows + KD :]
         w_buf[peer * KD : (peer + 1) * KD, :] = first[:, 0:R] + (first[:, R:] + last[:, 0:R])
     weights = w_buf[...]
     gram_buf[0:R, :] = lax.dot_general(
@@ -213,9 +217,6 @@
         wide_halves(gram_buf[pl.ds(w_first, w_rows), :]),
         wide_halves(gram_buf[pl.ds(v_first, v_rows), :]),
     ]
-    spare = out_ref.shape[1] - R // 2 - w_rows - v_rows
-    if spare:
-        parts.append(jnp.zeros((spare, 2 * R), jnp.float32))
     value = jnp.concatenate(parts, axis=0).astype(jnp.bfloat16)
     for peer in range(out_ref.shape[0]):
         out_ref[peer] = value
@@ -223,17 +224,16 @@
 
 def head_kernel(pack_ref, proj_ref, w_ref, newh_ref, hp_ref, col_ref, side_ref, *, sizes):
     ny, _, nc, nx = sizes
-    w_rows, v_rows = R // nx, R // (ny * nc)
-    head = jnp.zeros((R // 2, 2 * R), jnp.float32)
-    w_parts, v_parts = [0.0] * nx, [0.0] * (ny * nc)
+    h_rows, w_rows, v_rows = R // nx // 2, R // nx, R // (ny * nc)
+    w_last = h_rows + w_rows
+    h_parts, w_parts, v_parts = [0.0] * nx, [0.0] * nx, [0.0] * (ny * nc)
     for peer in range(pack_ref.shape[0]):
         value = pack_ref[peer].astype(jnp.float32)
         place, x = divmod(peer, nx)
-        w_last = R // 2 + w_rows
-        head = head + value[0 : R // 2]
-        w_parts[x] = w_parts[x] + value[R // 2 : w_last]
+        h_parts[x] = h_parts[x] + value[0:h_rows]
+        w_parts[x] = w_parts[x] + value[h_rows:w_last]
         v_parts[place] = v_parts[place] + value[w_last : w_last + v_rows]
-    head = unfold(head)
+    head = jnp.concatenate([unfold(part) for part in h_parts], axis=0)
     wgram, fgram = [
         jnp.concatenate([part[:, 0:R] + part[:, R:] for part in parts], axis=0) for parts in (w_parts, v_parts)
     ]
@@ -319,16 +319,17 @@
     parts = share(parts, "x", nx)
     proj, send = pl.pallas_call(
         functools.partial(polar_kernel, peers=nx),
-        in_specs=[pl.BlockSpec(memory_space=pltpu.SMEM)] * 2 + vmem(5),
+        in_specs=[pl.BlockSpec(memory_space=pltpu.SMEM)] * 2 + vmem(4),
         out_specs=vmem(2),
-        out_shape=[f32(R, KD * width), jax.ShapeDtypeStruct((R // 2 + 2 * KD, 2 * R), jnp.bfloat16)],
+        out_shape=[f32(R, KD * width), jax.ShapeDtypeStruct((R // nx // 2 + 2 * KD, 2 * R), jnp.bfloat16)],
         scratch_shapes=[
             pltpu.VMEM((KD * R, rows), jnp.bfloat16),
+            pltpu.VMEM((R, R), jnp.float32),
         ],
         compiler_params=params(),
-    )(tile_owner, lengths, parts, series, factor_h, factor_v, w_rows)
+    )(tile_owner, lengths, parts, series, factor_h, w_rows)
     near = ny * nc * nx
-    share_rows = -(-(R // 2 + R // nx + R // (ny * nc)) // 16) * 16
+    share_rows = R // nx // 2 + R // nx + R // (ny * nc)
     pieces = pl.pallas_call(
         functools.partial(middle_kernel, sizes=sizes),
         in_specs=vmem(2),

time: 127 us -> 122 us (0.961)
  blocking collectives: 109 us -> 104 us
    all_to_all x8, blocking collectives: 109 us -> 104 us  [exchange(): return lax.all_to_all(value, axes, 0, 0, tiled=True)]
where the time goes in v6:
time: 122 us
  blocking collectives  104 us (85%)
  Pallas kernels  16.8 us (14%)
    all_to_all x8, blocking collectives, exchange(): return lax.all_to_all(value, axes, 0, 0, tiled=True)  104 us
    pallas_call x1, Pallas kernels, body(): pl.pallas_call(functools.partial(polar_kernel, peers=nx), in_specs=[pl.Bl...  6.29 us
    pallas_call x1, Pallas kernels, body(): pl.pallas_call(functools.partial(head_kernel, sizes=sizes), in_specs=vmem...  3.98 us
    pallas_call x1, Pallas kernels, body(): pl.pallas_call(partial_kernel, in_specs=[pl.BlockSpec(memory_space=pltpu....  2.68 us

profile of v6, /device:TPU:1, one launch (start us, length us, event | category | flops | bytes accessed | tf_op | source)
XLA Modules:
  0.0 121.5 jit_solution(750961651929636169)
XLA Ops:
  0.6 2.7 %shard_map.85 = bf16[4,64,768]{2,1,0:T(8,128)(2,1)} custom-call(f32[64,256]{1,0:T(8,128)} %v_ref.3, bf16[3072,256]{1,0:T(8,128)(2,1)} %s_ref.3), custom_call_target="tpu_custom_call" | custom-call | tf_op jit(solution)/shard_map/pallas_call | solution.py:306
  3.3 0.0 copy-start
  3.3 0.0 copy-start.2
  3.3 0.0 copy-start.3
  3.4 0.0 copy-start.4
  3.4 0.0 copy-start.5
  3.4 11.2 %all_to_all.40 = bf16[4,64,768]{2,1,0:T(8,128)(2,1)S(1)} all-to-all(bf16[4,64,768]{2,1,0:T(8,128)(2,1)} %shard_map.85), channel_id=1, replica_groups=mesh['y'=4,'z'=16,'c'=2,'x'=4] {'x'}, dimensions={0} | all-to-all | bytes 786432 | tf_op jit(solution)/shard_map/all_to_all | solution.py:293
  14.6 0.1 reduce_sum.33
  14.7 0.0 copy-start.1
  14.7 8.8 %all_to_all.41.part_ref = bf16[4,64,768]{2,1,0:T(8,128)(2,1)S(1)} all-to-all(bf16[4,64,768]{2,1,0:T(8,128)(2,1)S(1)} %broadcast_in_dim.8), channel_id=1, replica_groups=mesh['y'=4,'z'=16,'c'=2,'x'=4] {'x'}, dimensions={0} | all-to-all | bytes 786432 | tf_op jit(solution)/shard_map/all_to_all | solution.py:293
  23.5 0.0 copy-done
  23.5 0.0 copy-done.2
  23.5 0.0 copy-done.3
  23.5 0.0 copy-done.4
  23.5 0.0 copy-done.5
  23.5 6.3 %shard_map.86 = (f32[64,1024]{1,0:T(8,128)S(1)}, bf16[16,128]{1,0:T(8,128)(2,1)S(1)}) custom-call(s32[24]{0:T(128)S(1)} %copy-done.4, s32[4]{0:T(128)S(1)} %copy-done.5, bf16[4,64,768]{2,1,0:T(8,128)(2,1)S(1)} %all_to_all.41.part_ref, bf16[3072,256]{1,0:T(8,128)(2,1)S(1)} %copy-done, f32[64,64]{1,0:T(8,128)S(1)} %copy-done.2, f32[4,64]{1,0:T(4,128)S(1)} %bitcast.6), custom_call_target="tpu_custom_call" | custom-call | tf_op jit(solution)/shard_map/pallas_call | solution.py:320
  29.8 27.2 %all_to_all.42.in_ref = bf16[16,16,128]{2,1,0:T(8,128)(2,1)S(1)} all-to-all(bf16[16,16,128]{2,1,0:T(8,128)(2,1)S(1)} %broadcast_in_dim.9), channel_id=1, replica_groups=mesh['y'=4,'z'=16,'c'=2,'x'=4] {'z'}, dimensions={0} | all-to-all | bytes 131072 | tf_op jit(solution)/shard_map/all_to_all | solution.py:293
  57.0 0.0 copy-done.1
  57.0 0.5 shard_map.87
  57.5 18.5 %all_to_all.43.pack_ref = bf16[32,32,128]{2,1,0:T(8,128)(2,1)S(1)} all-to-all(bf16[32,32,128]{2,1,0:T(8,128)(2,1)S(1)} %shard_map.87), channel_id=1, replica_groups=mesh['y'=4,'z'=16,'c'=2,'x'=4] {'y','c','x'}, dimensions={0} | all-to-all | bytes 524288 | tf_op jit(solution)/shard_map/all_to_all | solution.py:293
  76.1 4.0 %shard_map.88 = (f32[64,64]{1,0:T(8,128)}, f32[64,1024]{1,0:T(8,128)S(1)}, bf16[128,128]{1,0:T(8,128)(2,1)S(1)}, f32[64,128]{1,0:T(8,128)S(1)}) custom-call(bf16[32,32,128]{2,1,0:T(8,128)(2,1)S(1)} %all_to_all.43.pack_ref, f32[64,1024]{1,0:T(8,128)S(1)} %get-tuple-element.12.proj_ref, f32[4,64]{1,0:T(4,128)S(1)} %bitcast.7), custom_call_target="tpu_custom_call" | custom-call | tf_op jit(solution)/shard_map/pallas_call | solution.py:342
  80.0 7.4 %all_to_all.44 = bf16[8,16,128]{2,1,0:T(8,128)(2,1)S(1)} all-to-all(bf16[8,16,128]{2,1,0:T(8,128)(2,1)S(1)} %bitcast.5), channel_id=1, replica_groups=mesh['y'=4,'z'=16,'c'=2,'x'=4] {'y','c'}, dimensions={0} | all-to-all | bytes 65536 | tf_op jit(solution)/shard_map/all_to_all | solution.py:293
  87.5 14.2 %all_to_all.45 = bf16[16,16,128]{2,1,0:T(8,128)(2,1)S(1)} all-to-all(bf16[16,16,128]{2,1,0:T(8,128)(2,1)S(1)} %broadcast_in_dim.10), channel_id=1, replica_groups=mesh['y'=4,'z'=16,'c'=2,'x'=4] {'z'}, dimensions={0} | all-to-all | bytes 131072 | tf_op jit(solution)/shard_map/all_to_all | solution.py:293
  101.8 9.2 %all_to_all.46 = f32[8,16,128]{2,1,0:T(8,128)S(1)} all-to-all(f32[8,16,128]{2,1,0:T(8,128)S(1)} %broadcast_in_dim.11), channel_id=1, replica_groups=mesh['y'=4,'z'=16,'c'=2,'x'=4] {'y','c'}, dimensions={0} | all-to-all | bytes 131072 | tf_op jit(solution)/shard_map/all_to_all | solution.py:293
  111.0 0.9 shard_map.89
  111.9 7.2 %all_to_all.47.in_ref = f32[4,64,128]{2,1,0:T(8,128)S(1)} all-to-all(f32[4,64,128]{2,1,0:T(8,128)S(1)} %get-tuple-element.18), channel_id=1, replica_groups=mesh['y'=4,'z'=16,'c'=2,'x'=4] {'x'}, dimensions={0} | all-to-all | bytes 262144 | tf_op jit(solution)/shard_map/all_to_all | solution.py:293
  119.1 2.4 %shard_map.90 = f32[4,64]{1,0:T(4,128)} custom-call(f32[4,64,128]{2,1,0:T(8,128)S(1)} %all_to_all.47.in_ref, f32[64,128]{1,0:T(8,128)S(1)} %get-tuple-element.16.inverse_ref.side_ref), custom_call_target="tpu_custom_call" | custom-call | tf_op jit(solution)/shard_map/pallas_call | solution.py:360
  (6 shorter events, 0.1 us)
Async XLA Ops:
  3.3 20.1 %copy-start = (bf16[3072,256]{1,0:T(8,128)(2,1)S(1)}, bf16[3072,256]{1,0:T(8,128)(2,1)}, u32[]{:S(2)}) copy-start(bf16[3072,256]{1,0:T(8,128)(2,1)} %s_ref.3) | copy-start | bytes 4718596
  3.3 20.1 %copy-start.2 = (f32[64,64]{1,0:T(8,128)S(1)}, f32[64,64]{1,0:T(8,128)}, u32[]{:S(2)}) copy-start(f32[64,64]{1,0:T(8,128)} %h_ref.1) | copy-start | bytes 49156
  3.3 20.1 %copy-start.3 = (f32[64,4]{0,1:T(4,128)S(1)}, f32[64,4]{0,1:T(4,128)}, u32[]{:S(2)}) copy-start(f32[64,4]{0,1:T(4,128)} %param.11) | copy-start | bytes 3076
  3.4 20.1 %copy-start.4 = (s32[24]{0:T(128)S(1)}, s32[24]{0:T(128)}, u32[]{:S(2)}) copy-start(s32[24]{0:T(128)} %owner_ref.1) | copy-start | bytes 292
  3.4 20.1 %copy-start.5 = (s32[4]{0:T(128)S(1)}, s32[4]{0:T(128)}, u32[]{:S(2)}) copy-start(s32[4]{0:T(128)} %length_ref.1) | copy-start | bytes 52
  14.7 42.3 %copy-start.1 = (f32[64,256]{1,0:T(8,128)S(1)}, f32[64,256]{1,0:T(8,128)}, u32[]{:S(2)}) copy-start(f32[64,256]{1,0:T(8,128)} %v_ref.3) | copy-start | bytes 196612

commit v7 on v4

--- a/solution.py
+++ b/solution.py
@@ -77,7 +77,7 @@
     return both
 
 
-def partial_kernel(v_ref, s_ref, out_ref, v_buf, s_buf, sems):
+def partial_kernel(v_ref, s_ref, out_ref, planes_ref, v_buf, s_buf, sems):
     count, _, quarter = out_ref.shape
     pieces = 2
     step = count * quarter // pieces
@@ -88,7 +88,9 @@
     for copy in copies:
         copy.start()
     copies[0].wait()
-    factor_bf = v_buf[...].astype(jnp.bfloat16)
+    vmat = v_buf[...]
+    factor_bf = vmat.astype(jnp.bfloat16)
+    planes_ref[...] = wide_halves(mm_t(vmat, vmat)).astype(jnp.bfloat16)
     for i in range(pieces):
         copies[i + 1].wait()
         for peer in range(i * count // pieces, max((i + 1) * count // pieces, i * count // pieces + 1)):
@@ -105,7 +107,7 @@
 
 
 def polar_kernel(
-    owner_ref, length_ref, part_ref, s_ref, h_ref, v_ref, w_ref, proj_ref, pack_ref, p_ref, *, peers, spread
+    owner_ref, length_ref, part_ref, s_ref, h_ref, w_ref, proj_ref, send_ref, fgram_ref, p_ref, *, peers
 ):
     rows, width = s_ref.shape
     slots = rows // TILE
@@ -118,7 +120,12 @@
             first = first + jnp.where(owner_ref[t] < k, TILE, 0)
         live = (lane >= first) & (lane < first + length_ref[k])
         masks.append(jnp.where(live, 1.0, 0.0).astype(jnp.bfloat16))
-    summed = jnp.concatenate([part_ref[peer] for peer in range(peers)], axis=1)
+    base = rows // peers
+    summed = jnp.concatenate([part_ref[peer, :, 0:base] for peer in range(peers)], axis=1)
+    planes = part_ref[0, :, base:].astype(jnp.float32)
+    for peer in range(1, peers):
+        planes = planes + part_ref[peer, :, base:].astype(jnp.float32)
+    fgram_ref[...] = planes[:, 0:R] + planes[:, R:]
     for k in range(KD):
         p_ref[k * R : (k + 1) * R, :] = summed * masks[k]
     hmat = h_ref[...]
@@ -161,21 +168,59 @@
         for k in range(KD):
             p_ref[k * R : (k + 1) * R, cols] = polar * masks[k][:, cols]
     projected = jnp.dot(p_ref[...], s_ref[...], preferred_element_type=jnp.float32)
-    vmat = v_ref[...]
+    heads = lax.dot_general(p_ref[...], summed, LANES, preferred_element_type=jnp.float32)
     head = jnp.zeros((R, R), jnp.float32)
     for k in range(KD):
-        block = projected[k * R : (k + 1) * R, :]
-        proj_ref[:, k * width : (k + 1) * width] = block
-        head = head + mm_halves(block, vmat * wmat[:, k : k + 1], LANES)
-    pack_ref[0:R, :] = jnp.concatenate([head, mm_t(wmat, wmat) * (1.0 / peers)], axis=1)
-    pack_ref[R : 2 * R, :] = jnp.concatenate(
-        [mm_t(vmat, vmat) * (1.0 / spread), jnp.zeros((R, R), jnp.float32)], axis=1
-    )
-
-
-def head_kernel(pack_ref, proj_ref, w_ref, newh_ref, hp_ref, col_ref, side_ref):
-    head, wgram = pack_ref[0:R, 0:R], pack_ref[0:R, R : 2 * R]
-    fgram = pack_ref[R : 2 * R, 0:R]
+        proj_ref[:, k * width : (k + 1) * width] = projected[k * R : (k + 1) * R, :]
+        head = head + heads[k * R : (k + 1) * R, :] * column_rows[k]
+    high, middle, low = [term.astype(jnp.float32) for term in three(w_ref[...])]
+    send_ref[...] = jnp.concatenate(
+        [
+            fold(head),
+            jnp.concatenate([high, middle], axis=1),
+            jnp.concatenate([low, jnp.zeros_like(low)], axis=1),
+        ],
+        axis=0,
+    ).astype(jnp.bfloat16)
+
+
+def fold(value):
+    half = value.shape[0] // 2
+    return jnp.concatenate([value[0:half], value[half:]], axis=1)
+
+
+def unfold(value):
+    return jnp.concatenate([value[:, 0:R], value[:, R : 2 * R]], axis=0)
+
+
+def wide_halves(value):
+    return jnp.concatenate([half.astype(jnp.float32) for half in halves(value)], axis=1)
+
+
+def middle_kernel(in_ref, out_ref, w_buf):
+    half = R // 2
+    head = jnp.zeros((half, 2 * R), jnp.float32)
+    for peer in range(in_ref.shape[0]):
+        value = in_ref[peer].astype(jnp.float32)
+        head = head + value[0:half]
+        first, last = value[half : half + KD], value[half + KD :]
+        w_buf[peer * KD : (peer + 1) * KD, :] = first[:, 0:R] + (first[:, R:] + last[:, 0:R])
+    weights = w_buf[...]
+    wgram = lax.dot_general(
+        weights, weights, (((0,), (0,)), ((), ())), precision=highest, preferred_element_type=jnp.float32
+    )
+    value = jnp.concatenate([head, wide_halves(wgram)], axis=0).astype(jnp.bfloat16)
+    for peer in range(out_ref.shape[0]):
+        out_ref[peer] = value
+
+
+def head_kernel(pack_ref, fgram_ref, proj_ref, w_ref, newh_ref, hp_ref, col_ref, side_ref):
+    value = pack_ref[0].astype(jnp.float32)
+    for peer in range(1, pack_ref.shape[0]):
+        value = value + pack_ref[peer].astype(jnp.float32)
+    head = unfold(value[0 : R // 2])
+    wgram = value[R // 2 :, 0:R] + value[R // 2 :, R:]
+    fgram = fgram_ref[...]
     newh_t = eliminate(jnp.concatenate([fgram * wgram, head.T], axis=1))[:, R:]
     newh_ref[...] = newh_t.T
     wmat = w_ref[...].T
@@ -242,11 +287,14 @@
     slots = tile_owner.shape[0]
     quarter = rows // nx
     w_rows = weights_s.T
-    parts = pl.pallas_call(
+    parts, planes = pl.pallas_call(
         partial_kernel,
         in_specs=[pl.BlockSpec(memory_space=pltpu.HBM)] * 2,
-        out_specs=pl.BlockSpec(memory_space=pltpu.VMEM),
-        out_shape=jax.ShapeDtypeStruct((nx, R, quarter), jnp.bfloat16),
+        out_specs=vmem(2),
+        out_shape=[
+            jax.ShapeDtypeStruct((nx, R, quarter), jnp.bfloat16),
+            jax.ShapeDtypeStruct((R, 2 * R), jnp.bfloat16),
+        ],
         scratch_shapes=[
             pltpu.VMEM((R, width), jnp.float32),
             pltpu.VMEM((rows, width), jnp.bfloat16),
@@ -255,28 +303,38 @@
         compiler_params=params(63),
     )(factor_v, series)
     parts = jnp.sum(exchange(parts, "x").astype(jnp.float32), axis=0).astype(jnp.bfloat16)
-    parts = share(parts, "x", nx)
-    proj, pack = pl.pallas_call(
-        functools.partial(polar_kernel, peers=nx, spread=ny * nz * nc),
-        in_specs=[pl.BlockSpec(memory_space=pltpu.SMEM)] * 2 + vmem(5),
-        out_specs=vmem(2),
-        out_shape=[f32(R, KD * width), f32(2 * R, 2 * R)],
+    parts = share(jnp.concatenate([parts, planes], axis=1), "x", nx)
+    proj, send, fgram = pl.pallas_call(
+        functools.partial(polar_kernel, peers=nx),
+        in_specs=[pl.BlockSpec(memory_space=pltpu.SMEM)] * 2 + vmem(4),
+        out_specs=vmem(3),
+        out_shape=[
+            f32(R, KD * width),
+            jax.ShapeDtypeStruct((R // 2 + 2 * KD, 2 * R), jnp.bfloat16),
+            f32(R, R),
+        ],
         scratch_shapes=[
             pltpu.VMEM((KD * R, rows), jnp.bfloat16),
         ],
         compiler_params=params(),
-    )(tile_owner, lengths, parts, series, factor_h, factor_v, w_rows)
-    near = ny * nc * nx
-    pieces = exchange(pack.reshape(near, 2 * R // near, 2 * R), ("y", "c", "x"))
-    pieces = share(jnp.sum(pieces, axis=0), "z", nz)
-    pieces = share(jnp.sum(pieces, axis=0), ("y", "c", "x"), near)
+    )(tile_owner, lengths, parts, series, factor_h, w_rows)
+    near = ny * nc
+    pieces = pl.pallas_call(
+        middle_kernel,
+        in_specs=vmem(1),
+        out_specs=pl.BlockSpec(memory_space=pltpu.VMEM),
+        out_shape=jax.ShapeDtypeStruct((near, R // 2 + R, 2 * R), jnp.bfloat16),
+        scratch_shapes=[pltpu.VMEM((nz * KD, R), jnp.float32)],
+        compiler_params=params(),
+    )(share(send, "z", nz))
+    pieces = exchange(pieces, ("y", "c"))
     new_h, hp, col, side = pl.pallas_call(
         head_kernel,
-        in_specs=vmem(3),
+        in_specs=vmem(4),
         out_specs=vmem(4),
         out_shape=[f32(R, R), f32(R, KD * width), jax.ShapeDtypeStruct((R * width // TILE, TILE), jnp.bfloat16), f32(R, 2 * R)],
         compiler_params=params(),
-    )(pieces.reshape(2 * R, 2 * R), proj, w_rows)
+    )(pieces, fgram, proj, w_rows)
     near = ny * nc
     pieces = exchange(col.reshape(near, col.shape[0] // near, TILE), ("y", "c"))
     pieces = share(jnp.sum(pieces.astype(jnp.float32), axis=0).astype(jnp.bfloat16), "z", nz).astype(jnp.float32)

time: 131 us -> 122 us (0.931)
  blocking collectives: 113 us -> 103 us
    all_to_all x9 -> x8, blocking collectives: 113 us -> 103 us  [exchange(): return lax.all_to_all(value, axes, 0, 0, tiled=True)]
    pallas_call x2 -> x3, Pallas kernels: 10.4 us -> 10.7 us  [the longest x1 6.29 us: body(): pl.pallas_call(functools.partial(polar_kernel, peers=nx), in_specs=[pl.Bl...]
where the time goes in v7:
time: 122 us; the launch traced here: 121 us
  blocking collectives  103 us (84%)
  Pallas kernels  16.8 us (14%)
    all_to_all x8, blocking collectives, exchange(): return lax.all_to_all(value, axes, 0, 0, tiled=True)  103 us
    pallas_call x1, Pallas kernels, body(): pl.pallas_call(functools.partial(polar_kernel, peers=nx), in_specs=[pl.Bl...  6.29 us
    pallas_call x1, Pallas kernels, body(): pl.pallas_call(head_kernel, in_specs=vmem(4), out_specs=vmem(4), out_shap...  3.98 us
    pallas_call x1, Pallas kernels, body(): pl.pallas_call(partial_kernel, in_specs=[pl.BlockSpec(memory_space=pltpu....  2.73 us

profile of v7, /device:TPU:1, one launch (start us, length us, event | category | flops | bytes accessed | tf_op | source)
XLA Modules:
  0.0 121.4 jit_solution(6576831316292975536)
XLA Ops:
  0.6 2.7 %shard_map.85 = (bf16[4,64,768]{2,1,0:T(8,128)(2,1)}, bf16[64,128]{1,0:T(8,128)(2,1)}) custom-call(f32[64,256]{1,0:T(8,128)} %v_ref.1, bf16[3072,256]{1,0:T(8,128)(2,1)} %s_ref.3), custom_call_target="tpu_custom_call" | custom-call | tf_op jit(solution)/shard_map/pallas_call | solution.py:290
  3.4 0.0 copy-start
  3.4 0.0 copy-start.1
  3.4 0.0 copy-start.2
  3.4 0.0 copy-start.3
  3.4 0.0 copy-start.4
  3.4 11.2 %all_to_all.40 = bf16[4,64,768]{2,1,0:T(8,128)(2,1)S(1)} all-to-all(bf16[4,64,768]{2,1,0:T(8,128)(2,1)} %get-tuple-element.14), channel_id=1, replica_groups=mesh['y'=4,'z'=16,'c'=2,'x'=4] {'x'}, dimensions={0} | all-to-all | bytes 786432 | tf_op jit(solution)/shard_map/all_to_all | solution.py:277
  14.6 0.1 reduce_sum.33
  14.7 0.7 pad_maximum_fusion
  15.5 9.0 %all_to_all.41.part_ref = bf16[4,64,896]{2,1,0:T(8,128)(2,1)S(1)} all-to-all(bf16[4,64,896]{2,1,0:T(8,128)(2,1)S(1)} %broadcast_in_dim.8), channel_id=1, replica_groups=mesh['y'=4,'z'=16,'c'=2,'x'=4] {'x'}, dimensions={0} | all-to-all | bytes 917504 | tf_op jit(solution)/shard_map/all_to_all | solution.py:277
  24.4 0.0 copy-done
  24.4 0.0 copy-done.1
  24.4 0.0 copy-done.2
  24.5 0.0 copy-done.3
  24.5 0.0 copy-done.4
  24.5 6.3 %shard_map.86 = (f32[64,1024]{1,0:T(8,128)S(1)}, bf16[40,128]{1,0:T(8,128)(2,1)S(1)}, f32[64,64]{1,0:T(8,128)S(1)}) custom-call(s32[24]{0:T(128)S(1)} %copy-done.3, s32[4]{0:T(128)S(1)} %copy-done.4, bf16[4,64,896]{2,1,0:T(8,128)(2,1)S(1)} %all_to_all.41.part_ref, bf16[3072,256]{1,0:T(8,128)(2,1)S(1)} %copy-done, f32[64,64]{1,0:T(8,128)S(1)} %copy-done.1, ...), custom_call_target="tpu_custom_call" | custom-call | tf_op jit(solution)/shard_map/pallas_call | solution.py:307
  30.8 27.9 %all_to_all.42.in_ref = bf16[16,40,128]{2,1,0:T(8,128)(2,1)S(1)} all-to-all(bf16[16,40,128]{2,1,0:T(8,128)(2,1)S(1)} %broadcast_in_dim.9), channel_id=1, replica_groups=mesh['y'=4,'z'=16,'c'=2,'x'=4] {'z'}, dimensions={0} | all-to-all | bytes 327680 | tf_op jit(solution)/shard_map/all_to_all | solution.py:277
  58.7 0.5 shard_map.87
  59.1 14.8 %all_to_all.43.pack_ref = bf16[8,96,128]{2,1,0:T(8,128)(2,1)S(1)} all-to-all(bf16[8,96,128]{2,1,0:T(8,128)(2,1)S(1)} %shard_map.87), channel_id=1, replica_groups=mesh['y'=4,'z'=16,'c'=2,'x'=4] {'y','c'}, dimensions={0} | all-to-all | bytes 393216 | tf_op jit(solution)/shard_map/all_to_all | solution.py:277
  74.0 4.0 %shard_map.88 = (f32[64,64]{1,0:T(8,128)}, f32[64,1024]{1,0:T(8,128)S(1)}, bf16[128,128]{1,0:T(8,128)(2,1)S(1)}, f32[64,128]{1,0:T(8,128)S(1)}) custom-call(bf16[8,96,128]{2,1,0:T(8,128)(2,1)S(1)} %all_to_all.43.pack_ref, f32[64,64]{1,0:T(8,128)S(1)} %get-tuple-element.17.fgram_ref, f32[64,1024]{1,0:T(8,128)S(1)} %get-tuple-element.18.proj_ref, ...), custom_call_target="tpu_custom_call" | custom-call | tf_op jit(solution)/shard_map/pallas_call | solution.py:331
  78.0 8.0 %all_to_all.44 = bf16[8,16,128]{2,1,0:T(8,128)(2,1)S(1)} all-to-all(bf16[8,16,128]{2,1,0:T(8,128)(2,1)S(1)} %bitcast.5), channel_id=1, replica_groups=mesh['y'=4,'z'=16,'c'=2,'x'=4] {'y','c'}, dimensions={0} | all-to-all | bytes 65536 | tf_op jit(solution)/shard_map/all_to_all | solution.py:277
  86.0 15.4 %all_to_all.45 = bf16[16,16,128]{2,1,0:T(8,128)(2,1)S(1)} all-to-all(bf16[16,16,128]{2,1,0:T(8,128)(2,1)S(1)} %broadcast_in_dim.10), channel_id=1, replica_groups=mesh['y'=4,'z'=16,'c'=2,'x'=4] {'z'}, dimensions={0} | all-to-all | bytes 131072 | tf_op jit(solution)/shard_map/all_to_all | solution.py:277
  101.5 9.4 %all_to_all.46 = f32[8,16,128]{2,1,0:T(8,128)S(1)} all-to-all(f32[8,16,128]{2,1,0:T(8,128)S(1)} %broadcast_in_dim.11), channel_id=1, replica_groups=mesh['y'=4,'z'=16,'c'=2,'x'=4] {'y','c'}, dimensions={0} | all-to-all | bytes 131072 | tf_op jit(solution)/shard_map/all_to_all | solution.py:277
  110.9 0.9 shard_map.89
  111.8 7.2 %all_to_all.47.in_ref = f32[4,64,128]{2,1,0:T(8,128)S(1)} all-to-all(f32[4,64,128]{2,1,0:T(8,128)S(1)} %get-tuple-element.24), channel_id=1, replica_groups=mesh['y'=4,'z'=16,'c'=2,'x'=4] {'x'}, dimensions={0} | all-to-all | bytes 262144 | tf_op jit(solution)/shard_map/all_to_all | solution.py:277
  119.0 2.4 %shard_map.90 = f32[4,64]{1,0:T(4,128)} custom-call(f32[4,64,128]{2,1,0:T(8,128)S(1)} %all_to_all.47.in_ref, f32[64,128]{1,0:T(8,128)S(1)} %get-tuple-element.22.inverse_ref.side_ref), custom_call_target="tpu_custom_call" | custom-call | tf_op jit(solution)/shard_map/pallas_call | solution.py:349
  (6 shorter events, 0.1 us)
Async XLA Ops:
  3.4 21.1 %copy-start = (bf16[3072,256]{1,0:T(8,128)(2,1)S(1)}, bf16[3072,256]{1,0:T(8,128)(2,1)}, u32[]{:S(2)}) copy-start(bf16[3072,256]{1,0:T(8,128)(2,1)} %s_ref.3) | copy-start | bytes 4718596
  3.4 21.1 %copy-start.1 = (f32[64,64]{1,0:T(8,128)S(1)}, f32[64,64]{1,0:T(8,128)}, u32[]{:S(2)}) copy-start(f32[64,64]{1,0:T(8,128)} %h_ref.1) | copy-start | bytes 49156
  3.4 21.1 %copy-start.2 = (f32[64,4]{0,1:T(4,128)S(1)}, f32[64,4]{0,1:T(4,128)}, u32[]{:S(2)}) copy-start(f32[64,4]{0,1:T(4,128)} %param.11) | copy-start | bytes 3076
  3.4 21.1 %copy-start.3 = (s32[24]{0:T(128)S(1)}, s32[24]{0:T(128)}, u32[]{:S(2)}) copy-start(s32[24]{0:T(128)} %owner_ref.1) | copy-start | bytes 292
  3.4 21.1 %copy-start.4 = (s32[4]{0:T(128)S(1)}, s32[4]{0:T(128)}, u32[]{:S(2)}) copy-start(s32[4]{0:T(128)} %length_ref.1) | copy-start | bytes 52

commit v8 on v6

--- a/solution.py
+++ b/solution.py
@@ -105,9 +105,9 @@
 
 
 def polar_kernel(
-    owner_ref, length_ref, part_ref, s_ref, h_ref, w_ref, proj_ref, send_ref, p_ref, head_buf, *, peers
+    owner_ref, length_ref, part_ref, h_ref, w_ref, p_ref, send_ref, head_buf, *, peers
 ):
-    rows, width = s_ref.shape
+    rows = p_ref.shape[1]
     slots = rows // TILE
     eye = eye_mask()
     lane = lax.broadcasted_iota(jnp.int32, (1, rows), 1)
@@ -160,11 +160,9 @@
         polar = (terms[0:R] + (terms[R : 2 * R] + terms[2 * R : 3 * R])).astype(jnp.bfloat16)
         for k in range(KD):
             p_ref[k * R : (k + 1) * R, cols] = polar * masks[k][:, cols]
-    projected = jnp.dot(p_ref[...], s_ref[...], preferred_element_type=jnp.float32)
     heads = lax.dot_general(p_ref[...], summed, LANES, preferred_element_type=jnp.float32)
     head = jnp.zeros((R, R), jnp.float32)
     for k in range(KD):
-        proj_ref[:, k * width : (k + 1) * width] = projected[k * R : (k + 1) * R, :]
         head = head + heads[k * R : (k + 1) * R, :] * column_rows[k]
     head_buf[...] = head
     share_rows = R // peers
@@ -222,7 +220,7 @@
         out_ref[peer] = value
 
 
-def head_kernel(pack_ref, proj_ref, w_ref, newh_ref, hp_ref, col_ref, side_ref, *, sizes):
+def head_kernel(pack_ref, p_ref, s_ref, w_ref, newh_ref, hp_ref, col_ref, side_ref, *, sizes):
     ny, _, nc, nx = sizes
     h_rows, w_rows, v_rows = R // nx // 2, R // nx, R // (ny * nc)
     w_last = h_rows + w_rows
@@ -240,9 +238,11 @@
     newh_t = eliminate(jnp.concatenate([fgram * wgram, head.T], axis=1))[:, R:]
     newh_ref[...] = newh_t.T
     wmat = w_ref[...].T
-    hp = mm_halves(newh_t, proj_ref[...])
+    projected = jnp.dot(p_ref[...], s_ref[...], preferred_element_type=jnp.float32)
+    width = projected.shape[1]
+    projected = jnp.concatenate([projected[k * R : (k + 1) * R, :] for k in range(KD)], axis=1)
+    hp = mm_halves(newh_t, projected)
     hp_ref[...] = hp
-    width = hp.shape[1] // KD
     col = hp[:, 0:width] * wmat[:, 0:1]
     for k in range(1, KD):
         col = col + hp[:, k * width : (k + 1) * width] * wmat[:, k : k + 1]
@@ -259,12 +259,15 @@
     newv = mm(inverse_ref[:, R : 2 * R], col)
     newv_ref[...] = newv
     width = newv.shape[1]
-    lane = lax.broadcasted_iota(jnp.int32, (R, R), 1)
-    terms = jnp.zeros((R, R), jnp.float32)
+    eye = eye_mask()
+    row = lax.broadcasted_iota(jnp.int32, (8, R), 0)
+    terms = jnp.zeros((8, R), jnp.float32)
     for k in range(KD):
         sums = jnp.sum(hp_ref[:, k * width : (k + 1) * width] * newv, axis=1, keepdims=True)
-        terms = jnp.where(lane == k, sums, terms)
-    value = jnp.concatenate([mm_t(newv, newv), terms], axis=1)
+        terms = jnp.where(row == k, jnp.sum(jnp.where(eye, sums, 0.0), axis=0, keepdims=True), terms)
+    value = jnp.concatenate(
+        [fold(mm_t(newv, newv)), jnp.concatenate([terms, jnp.zeros_like(terms)], axis=1)], axis=0
+    )
     for peer in range(out_ref.shape[0]):
         out_ref[peer] = value
 
@@ -273,7 +276,9 @@
     value = in_ref[0]
     for peer in range(1, in_ref.shape[0]):
         value = value + in_ref[peer]
-    solved = eliminate(jnp.concatenate([side_ref[:, 0:R] * value[:, 0:R], value[:, R : 2 * R]], axis=1))
+    gram = side_ref[:, 0:R] * unfold(value[0 : R // 2])
+    terms = value[R // 2 :, 0:R].T
+    solved = eliminate(jnp.concatenate([gram, terms, jnp.zeros((R, R - 8), jnp.float32)], axis=1))
     out_ref[...] = solved[:, R : R + KD].T
 
 
@@ -317,17 +322,19 @@
     )(factor_v, series)
     parts = jnp.sum(exchange(parts, "x").astype(jnp.float32), axis=0).astype(jnp.bfloat16)
     parts = share(parts, "x", nx)
-    proj, send = pl.pallas_call(
+    polar, send = pl.pallas_call(
         functools.partial(polar_kernel, peers=nx),
-        in_specs=[pl.BlockSpec(memory_space=pltpu.SMEM)] * 2 + vmem(4),
+        in_specs=[pl.BlockSpec(memory_space=pltpu.SMEM)] * 2 + vmem(3),
         out_specs=vmem(2),
-        out_shape=[f32(R, KD * width), jax.ShapeDtypeStruct((R // nx // 2 + 2 * KD, 2 * R), jnp.bfloat16)],
+        out_shape=[
+            jax.ShapeDtypeStruct((KD * R, rows), jnp.bfloat16),
+            jax.ShapeDtypeStruct((R // nx // 2 + 2 * KD, 2 * R), jnp.bfloat16),
+        ],
         scratch_shapes=[
-            pltpu.VMEM((KD * R, rows), jnp.bfloat16),
             pltpu.VMEM((R, R), jnp.float32),
         ],
         compiler_params=params(),
-    )(tile_owner, lengths, parts, series, factor_h, w_rows)
+    )(tile_owner, lengths, parts, factor_h, w_rows)
     near = ny * nc * nx
     share_rows = R // nx // 2 + R // nx + R // (ny * nc)
     pieces = pl.pallas_call(
@@ -341,11 +348,11 @@
     pieces = exchange(pieces, ("y", "c", "x"))
     new_h, hp, col, side = pl.pallas_call(
         functools.partial(head_kernel, sizes=sizes),
-        in_specs=vmem(3),
+        in_specs=vmem(4),
         out_specs=vmem(4),
         out_shape=[f32(R, R), f32(R, KD * width), jax.ShapeDtypeStruct((R * width // TILE, TILE), jnp.bfloat16), f32(R, 2 * R)],
         compiler_params=params(),
-    )(pieces, proj, w_rows)
+    )(pieces, polar, series, w_rows)
     near = ny * nc
     pieces = exchange(col.reshape(near, col.shape[0] // near, TILE), ("y", "c"))
     pieces = share(jnp.sum(pieces.astype(jnp.float32), axis=0).astype(jnp.bfloat16), "z", nz).astype(jnp.float32)
@@ -354,7 +361,7 @@
         column_kernel,
         in_specs=vmem(3),
         out_specs=vmem(2),
-        out_shape=[f32(R, width), f32(nx, R, 2 * R)],
+        out_shape=[f32(R, width), f32(nx, R // 2 + 8, 2 * R)],
         compiler_params=params(),
     )(pieces.reshape(col.shape), hp, side)
     new_s = pl.pallas_call(

time: 122 us -> 122 us (level)
  no operation moved by 1% of the time
where the time goes in v8:
time: 122 us; the launch traced here: 121 us
  blocking collectives  104 us (85%)
  Pallas kernels  16.9 us (14%)
    all_to_all x8, blocking collectives, exchange(): return lax.all_to_all(value, axes, 0, 0, tiled=True)  104 us
    pallas_call x1, Pallas kernels, body(): pl.pallas_call(functools.partial(polar_kernel, peers=nx), in_specs=[pl.Bl...  5.93 us
    pallas_call x1, Pallas kernels, body(): pl.pallas_call(functools.partial(head_kernel, sizes=sizes), in_specs=vmem...  4.38 us
    pallas_call x1, Pallas kernels, body(): pl.pallas_call(partial_kernel, in_specs=[pl.BlockSpec(memory_space=pltpu....  2.68 us
    pallas_call x1, Pallas kernels, body(): pl.pallas_call(weight_kernel, in_specs=vmem(2), out_specs=pl.BlockSpec(me...  2.48 us

profile of v8, /device:TPU:1, one launch (start us, length us, event | category | flops | bytes accessed | tf_op | source)
XLA Modules:
  0.0 121.3 jit_solution(1726390655270784795)
XLA Ops:
  0.6 2.7 %shard_map.85 = bf16[4,64,768]{2,1,0:T(8,128)(2,1)} custom-call(f32[64,256]{1,0:T(8,128)} %v_ref.3, bf16[3072,256]{1,0:T(8,128)(2,1)} %s_ref.3), custom_call_target="tpu_custom_call" | custom-call | tf_op jit(solution)/shard_map/pallas_call | solution.py:311
  3.3 0.0 copy-start.2
  3.3 0.0 copy-start.3
  3.3 0.0 copy-start.4
  3.4 0.0 copy-start.5
  3.4 0.0 copy-start.1
  3.4 11.2 %all_to_all.40 = bf16[4,64,768]{2,1,0:T(8,128)(2,1)S(1)} all-to-all(bf16[4,64,768]{2,1,0:T(8,128)(2,1)} %shard_map.85), channel_id=1, replica_groups=mesh['y'=4,'z'=16,'c'=2,'x'=4] {'x'}, dimensions={0} | all-to-all | bytes 786432 | tf_op jit(solution)/shard_map/all_to_all | solution.py:298
  14.6 0.0 copy-start
  14.6 0.1 reduce_sum.33
  14.7 8.8 %all_to_all.41.part_ref = bf16[4,64,768]{2,1,0:T(8,128)(2,1)S(1)} all-to-all(bf16[4,64,768]{2,1,0:T(8,128)(2,1)S(1)} %broadcast_in_dim.8), channel_id=1, replica_groups=mesh['y'=4,'z'=16,'c'=2,'x'=4] {'x'}, dimensions={0} | all-to-all | bytes 786432 | tf_op jit(solution)/shard_map/all_to_all | solution.py:298
  23.5 0.0 copy-done.2
  23.5 0.0 copy-done.3
  23.5 0.0 copy-done.4
  23.5 0.0 copy-done.5
  23.5 5.9 %shard_map.86 = (bf16[256,3072]{1,0:T(8,128)(2,1)S(1)}, bf16[16,128]{1,0:T(8,128)(2,1)S(1)}) custom-call(s32[24]{0:T(128)S(1)} %copy-done.4, s32[4]{0:T(128)S(1)} %copy-done.5, bf16[4,64,768]{2,1,0:T(8,128)(2,1)S(1)} %all_to_all.41.part_ref, f32[64,64]{1,0:T(8,128)S(1)} %copy-done.2, f32[4,64]{1,0:T(4,128)S(1)} %bitcast.6), custom_call_target="tpu_custom_call" | custom-call | tf_op jit(solution)/shard_map/pallas_call | solution.py:325
  29.4 27.2 %all_to_all.42.in_ref = bf16[16,16,128]{2,1,0:T(8,128)(2,1)S(1)} all-to-all(bf16[16,16,128]{2,1,0:T(8,128)(2,1)S(1)} %broadcast_in_dim.9), channel_id=1, replica_groups=mesh['y'=4,'z'=16,'c'=2,'x'=4] {'z'}, dimensions={0} | all-to-all | bytes 131072 | tf_op jit(solution)/shard_map/all_to_all | solution.py:298
  56.6 0.0 copy-done.1
  56.6 0.5 shard_map.87
  57.2 18.5 %all_to_all.43.pack_ref = bf16[32,32,128]{2,1,0:T(8,128)(2,1)S(1)} all-to-all(bf16[32,32,128]{2,1,0:T(8,128)(2,1)S(1)} %shard_map.87), channel_id=1, replica_groups=mesh['y'=4,'z'=16,'c'=2,'x'=4] {'y','c','x'}, dimensions={0} | all-to-all | bytes 524288 | tf_op jit(solution)/shard_map/all_to_all | solution.py:298
  75.7 0.0 copy-done
  75.7 4.4 %shard_map.88 = (f32[64,64]{1,0:T(8,128)}, f32[64,1024]{1,0:T(8,128)S(1)}, bf16[128,128]{1,0:T(8,128)(2,1)S(1)}, f32[64,128]{1,0:T(8,128)S(1)}) custom-call(bf16[32,32,128]{2,1,0:T(8,128)(2,1)S(1)} %all_to_all.43.pack_ref, bf16[256,3072]{1,0:T(8,128)(2,1)S(1)} %get-tuple-element.12.p_ref, bf16[3072,256]{1,0:T(8,128)(2,1)S(1)} %copy-done, f32[4,64]{1,0:T(4,128)S(1)} %bitcast.7), custom_call_target="tpu_custom_call" | custom-call | tf_op jit(solution)/shard_map/pallas_call | solution.py:349
  80.1 7.4 %all_to_all.44 = bf16[8,16,128]{2,1,0:T(8,128)(2,1)S(1)} all-to-all(bf16[8,16,128]{2,1,0:T(8,128)(2,1)S(1)} %bitcast.5), channel_id=1, replica_groups=mesh['y'=4,'z'=16,'c'=2,'x'=4] {'y','c'}, dimensions={0} | all-to-all | bytes 65536 | tf_op jit(solution)/shard_map/all_to_all | solution.py:298
  87.5 14.2 %all_to_all.45 = bf16[16,16,128]{2,1,0:T(8,128)(2,1)S(1)} all-to-all(bf16[16,16,128]{2,1,0:T(8,128)(2,1)S(1)} %broadcast_in_dim.10), channel_id=1, replica_groups=mesh['y'=4,'z'=16,'c'=2,'x'=4] {'z'}, dimensions={0} | all-to-all | bytes 131072 | tf_op jit(solution)/shard_map/all_to_all | solution.py:298
  101.8 9.2 %all_to_all.46 = f32[8,16,128]{2,1,0:T(8,128)S(1)} all-to-all(f32[8,16,128]{2,1,0:T(8,128)S(1)} %broadcast_in_dim.11), channel_id=1, replica_groups=mesh['y'=4,'z'=16,'c'=2,'x'=4] {'y','c'}, dimensions={0} | all-to-all | bytes 131072 | tf_op jit(solution)/shard_map/all_to_all | solution.py:298
  111.0 0.9 shard_map.89
  111.9 6.9 %all_to_all.47.in_ref = f32[4,40,128]{2,1,0:T(8,128)S(1)} all-to-all(f32[4,40,128]{2,1,0:T(8,128)S(1)} %get-tuple-element.18), channel_id=1, replica_groups=mesh['y'=4,'z'=16,'c'=2,'x'=4] {'x'}, dimensions={0} | all-to-all | bytes 163840 | tf_op jit(solution)/shard_map/all_to_all | solution.py:298
  118.9 2.5 %shard_map.90 = f32[4,64]{1,0:T(4,128)} custom-call(f32[4,40,128]{2,1,0:T(8,128)S(1)} %all_to_all.47.in_ref, f32[64,128]{1,0:T(8,128)S(1)} %get-tuple-element.16.inverse_ref.side_ref), custom_call_target="tpu_custom_call" | custom-call | tf_op jit(solution)/shard_map/pallas_call | solution.py:367
  (6 shorter events, 0.1 us)
Async XLA Ops:
  3.3 20.1 %copy-start.2 = (f32[64,64]{1,0:T(8,128)S(1)}, f32[64,64]{1,0:T(8,128)}, u32[]{:S(2)}) copy-start(f32[64,64]{1,0:T(8,128)} %h_ref.1) | copy-start | bytes 49156
  3.3 20.1 %copy-start.3 = (f32[64,4]{0,1:T(4,128)S(1)}, f32[64,4]{0,1:T(4,128)}, u32[]{:S(2)}) copy-start(f32[64,4]{0,1:T(4,128)} %param.11) | copy-start | bytes 3076
  3.3 20.1 %copy-start.4 = (s32[24]{0:T(128)S(1)}, s32[24]{0:T(128)}, u32[]{:S(2)}) copy-start(s32[24]{0:T(128)} %owner_ref.1) | copy-start | bytes 292
  3.4 20.1 %copy-start.5 = (s32[4]{0:T(128)S(1)}, s32[4]{0:T(128)}, u32[]{:S(2)}) copy-start(s32[4]{0:T(128)} %length_ref.1) | copy-start | bytes 52
  3.4 53.3 %copy-start.1 = (f32[64,256]{1,0:T(8,128)S(1)}, f32[64,256]{1,0:T(8,128)}, u32[]{:S(2)}) copy-start(f32[64,256]{1,0:T(8,128)} %v_ref.3) | copy-start | bytes 196612
  14.6 61.1 %copy-start = (bf16[3072,256]{1,0:T(8,128)(2,1)S(1)}, bf16[3072,256]{1,0:T(8,128)(2,1)}, u32[]{:S(2)}) copy-start(bf16[3072,256]{1,0:T(8,128)(2,1)} %s_ref.3) | copy-start | bytes 4718596

commit v9 on v6

--- a/solution.py
+++ b/solution.py
@@ -259,12 +259,15 @@
     newv = mm(inverse_ref[:, R : 2 * R], col)
     newv_ref[...] = newv
     width = newv.shape[1]
-    lane = lax.broadcasted_iota(jnp.int32, (R, R), 1)
-    terms = jnp.zeros((R, R), jnp.float32)
+    eye = eye_mask()
+    row = lax.broadcasted_iota(jnp.int32, (8, R), 0)
+    terms = jnp.zeros((8, R), jnp.float32)
     for k in range(KD):
         sums = jnp.sum(hp_ref[:, k * width : (k + 1) * width] * newv, axis=1, keepdims=True)
-        terms = jnp.where(lane == k, sums, terms)
-    value = jnp.concatenate([mm_t(newv, newv), terms], axis=1)
+        terms = jnp.where(row == k, jnp.sum(jnp.where(eye, sums, 0.0), axis=0, keepdims=True), terms)
+    value = jnp.concatenate(
+        [fold(mm_t(newv, newv)), jnp.concatenate([terms, jnp.zeros_like(terms)], axis=1)], axis=0
+    )
     for peer in range(out_ref.shape[0]):
         out_ref[peer] = value
 
@@ -273,7 +276,9 @@
     value = in_ref[0]
     for peer in range(1, in_ref.shape[0]):
         value = value + in_ref[peer]
-    solved = eliminate(jnp.concatenate([side_ref[:, 0:R] * value[:, 0:R], value[:, R : 2 * R]], axis=1))
+    gram = side_ref[:, 0:R] * unfold(value[0 : R // 2])
+    terms = value[R // 2 :, 0:R].T
+    solved = eliminate(jnp.concatenate([gram, terms, jnp.zeros((R, R - 8), jnp.float32)], axis=1))
     out_ref[...] = solved[:, R : R + KD].T
 
 
@@ -354,7 +359,7 @@
         column_kernel,
         in_specs=vmem(3),
         out_specs=vmem(2),
-        out_shape=[f32(R, width), f32(nx, R, 2 * R)],
+        out_shape=[f32(R, width), f32(nx, R // 2 + 8, 2 * R)],
         compiler_params=params(),
     )(pieces.reshape(col.shape), hp, side)
     new_s = pl.pallas_call(

time: 122 us -> 122 us (level)
  no operation moved by 1% of the time
where the time goes in v9:
time: 122 us; the launch traced here: 121 us
  blocking collectives  104 us (85%)
  Pallas kernels  16.9 us (14%)
    all_to_all x8, blocking collectives, exchange(): return lax.all_to_all(value, axes, 0, 0, tiled=True)  104 us
    pallas_call x1, Pallas kernels, body(): pl.pallas_call(functools.partial(polar_kernel, peers=nx), in_specs=[pl.Bl...  6.29 us
    pallas_call x1, Pallas kernels, body(): pl.pallas_call(functools.partial(head_kernel, sizes=sizes), in_specs=vmem...  3.98 us
    pallas_call x1, Pallas kernels, body(): pl.pallas_call(partial_kernel, in_specs=[pl.BlockSpec(memory_space=pltpu....  2.68 us
    pallas_call x1, Pallas kernels, body(): pl.pallas_call(weight_kernel, in_specs=vmem(2), out_specs=pl.BlockSpec(me...  2.48 us

profile of v9, /device:TPU:1, one launch (start us, length us, event | category | flops | bytes accessed | tf_op | source)
XLA Modules:
  0.0 121.3 jit_solution(16872239225842928910)
XLA Ops:
  0.6 2.7 %shard_map.85 = bf16[4,64,768]{2,1,0:T(8,128)(2,1)} custom-call(f32[64,256]{1,0:T(8,128)} %v_ref.3, bf16[3072,256]{1,0:T(8,128)(2,1)} %s_ref.3), custom_call_target="tpu_custom_call" | custom-call | tf_op jit(solution)/shard_map/pallas_call | solution.py:311
  3.3 0.0 copy-start
  3.3 0.0 copy-start.2
  3.3 0.0 copy-start.3
  3.4 0.0 copy-start.4
  3.4 0.0 copy-start.5
  3.4 11.2 %all_to_all.40 = bf16[4,64,768]{2,1,0:T(8,128)(2,1)S(1)} all-to-all(bf16[4,64,768]{2,1,0:T(8,128)(2,1)} %shard_map.85), channel_id=1, replica_groups=mesh['y'=4,'z'=16,'c'=2,'x'=4] {'x'}, dimensions={0} | all-to-all | bytes 786432 | tf_op jit(solution)/shard_map/all_to_all | solution.py:298
  14.6 0.1 reduce_sum.33
  14.7 0.0 copy-start.1
  14.7 8.8 %all_to_all.41.part_ref = bf16[4,64,768]{2,1,0:T(8,128)(2,1)S(1)} all-to-all(bf16[4,64,768]{2,1,0:T(8,128)(2,1)S(1)} %broadcast_in_dim.8), channel_id=1, replica_groups=mesh['y'=4,'z'=16,'c'=2,'x'=4] {'x'}, dimensions={0} | all-to-all | bytes 786432 | tf_op jit(solution)/shard_map/all_to_all | solution.py:298
  23.5 0.0 copy-done
  23.5 0.0 copy-done.2
  23.5 0.0 copy-done.3
  23.5 0.0 copy-done.4
  23.5 0.0 copy-done.5
  23.5 6.3 %shard_map.86 = (f32[64,1024]{1,0:T(8,128)S(1)}, bf16[16,128]{1,0:T(8,128)(2,1)S(1)}) custom-call(s32[24]{0:T(128)S(1)} %copy-done.4, s32[4]{0:T(128)S(1)} %copy-done.5, bf16[4,64,768]{2,1,0:T(8,128)(2,1)S(1)} %all_to_all.41.part_ref, bf16[3072,256]{1,0:T(8,128)(2,1)S(1)} %copy-done, f32[64,64]{1,0:T(8,128)S(1)} %copy-done.2, f32[4,64]{1,0:T(4,128)S(1)} %bitcast.6), custom_call_target="tpu_custom_call" | custom-call | tf_op jit(solution)/shard_map/pallas_call | solution.py:325
  29.8 27.2 %all_to_all.42.in_ref = bf16[16,16,128]{2,1,0:T(8,128)(2,1)S(1)} all-to-all(bf16[16,16,128]{2,1,0:T(8,128)(2,1)S(1)} %broadcast_in_dim.9), channel_id=1, replica_groups=mesh['y'=4,'z'=16,'c'=2,'x'=4] {'z'}, dimensions={0} | all-to-all | bytes 131072 | tf_op jit(solution)/shard_map/all_to_all | solution.py:298
  57.0 0.0 copy-done.1
  57.0 0.5 shard_map.87
  57.5 18.5 %all_to_all.43.pack_ref = bf16[32,32,128]{2,1,0:T(8,128)(2,1)S(1)} all-to-all(bf16[32,32,128]{2,1,0:T(8,128)(2,1)S(1)} %shard_map.87), channel_id=1, replica_groups=mesh['y'=4,'z'=16,'c'=2,'x'=4] {'y','c','x'}, dimensions={0} | all-to-all | bytes 524288 | tf_op jit(solution)/shard_map/all_to_all | solution.py:298
  76.1 4.0 %shard_map.88 = (f32[64,64]{1,0:T(8,128)}, f32[64,1024]{1,0:T(8,128)S(1)}, bf16[128,128]{1,0:T(8,128)(2,1)S(1)}, f32[64,128]{1,0:T(8,128)S(1)}) custom-call(bf16[32,32,128]{2,1,0:T(8,128)(2,1)S(1)} %all_to_all.43.pack_ref, f32[64,1024]{1,0:T(8,128)S(1)} %get-tuple-element.12.proj_ref, f32[4,64]{1,0:T(4,128)S(1)} %bitcast.7), custom_call_target="tpu_custom_call" | custom-call | tf_op jit(solution)/shard_map/pallas_call | solution.py:347
  80.0 7.4 %all_to_all.44 = bf16[8,16,128]{2,1,0:T(8,128)(2,1)S(1)} all-to-all(bf16[8,16,128]{2,1,0:T(8,128)(2,1)S(1)} %bitcast.5), channel_id=1, replica_groups=mesh['y'=4,'z'=16,'c'=2,'x'=4] {'y','c'}, dimensions={0} | all-to-all | bytes 65536 | tf_op jit(solution)/shard_map/all_to_all | solution.py:298
  87.5 14.2 %all_to_all.45 = bf16[16,16,128]{2,1,0:T(8,128)(2,1)S(1)} all-to-all(bf16[16,16,128]{2,1,0:T(8,128)(2,1)S(1)} %broadcast_in_dim.10), channel_id=1, replica_groups=mesh['y'=4,'z'=16,'c'=2,'x'=4] {'z'}, dimensions={0} | all-to-all | bytes 131072 | tf_op jit(solution)/shard_map/all_to_all | solution.py:298
  101.8 9.2 %all_to_all.46 = f32[8,16,128]{2,1,0:T(8,128)S(1)} all-to-all(f32[8,16,128]{2,1,0:T(8,128)S(1)} %broadcast_in_dim.11), channel_id=1, replica_groups=mesh['y'=4,'z'=16,'c'=2,'x'=4] {'y','c'}, dimensions={0} | all-to-all | bytes 131072 | tf_op jit(solution)/shard_map/all_to_all | solution.py:298
  111.0 0.9 shard_map.89
  111.9 6.9 %all_to_all.47.in_ref = f32[4,40,128]{2,1,0:T(8,128)S(1)} all-to-all(f32[4,40,128]{2,1,0:T(8,128)S(1)} %get-tuple-element.18), channel_id=1, replica_groups=mesh['y'=4,'z'=16,'c'=2,'x'=4] {'x'}, dimensions={0} | all-to-all | bytes 163840 | tf_op jit(solution)/shard_map/all_to_all | solution.py:298
  118.8 2.5 %shard_map.90 = f32[4,64]{1,0:T(4,128)} custom-call(f32[4,40,128]{2,1,0:T(8,128)S(1)} %all_to_all.47.in_ref, f32[64,128]{1,0:T(8,128)S(1)} %get-tuple-element.16.inverse_ref.side_ref), custom_call_target="tpu_custom_call" | custom-call | tf_op jit(solution)/shard_map/pallas_call | solution.py:365
  (6 shorter events, 0.1 us)
Async XLA Ops:
  3.3 20.1 %copy-start = (bf16[3072,256]{1,0:T(8,128)(2,1)S(1)}, bf16[3072,256]{1,0:T(8,128)(2,1)}, u32[]{:S(2)}) copy-start(bf16[3072,256]{1,0:T(8,128)(2,1)} %s_ref.3) | copy-start | bytes 4718596
  3.3 20.1 %copy-start.2 = (f32[64,64]{1,0:T(8,128)S(1)}, f32[64,64]{1,0:T(8,128)}, u32[]{:S(2)}) copy-start(f32[64,64]{1,0:T(8,128)} %h_ref.1) | copy-start | bytes 49156
  3.3 20.1 %copy-start.3 = (f32[64,4]{0,1:T(4,128)S(1)}, f32[64,4]{0,1:T(4,128)}, u32[]{:S(2)}) copy-start(f32[64,4]{0,1:T(4,128)} %param.11) | copy-start | bytes 3076
  3.4 20.1 %copy-start.4 = (s32[24]{0:T(128)S(1)}, s32[24]{0:T(128)}, u32[]{:S(2)}) copy-start(s32[24]{0:T(128)} %owner_ref.1) | copy-start | bytes 292
  3.4 20.1 %copy-start.5 = (s32[4]{0:T(128)S(1)}, s32[4]{0:T(128)}, u32[]{:S(2)}) copy-start(s32[4]{0:T(128)} %length_ref.1) | copy-start | bytes 52
  14.7 42.3 %copy-start.1 = (f32[64,256]{1,0:T(8,128)S(1)}, f32[64,256]{1,0:T(8,128)}, u32[]{:S(2)}) copy-start(f32[64,256]{1,0:T(8,128)} %v_ref.3) | copy-start | bytes 196612
